TPU v7x, 32 devices: a whole 2x2x4 slice. The times are simulated.
32 devices in a mesh: dp: 16 (over z, y, x), group: 2 (over core).
Axes of the slice: x: 2, y: 2, z: 4, core: 2. Of those that a mesh axis runs over, the one named last changes fastest.
Arguments:
- queries: bfloat16 [12288, 4096], P('dp', 'group'), may hold values from -120 to 120
- passages: bfloat16 [12288, 4096], P('dp', 'group'), may hold values from -120 to 120
- neg_owner: int32 [12288, 8], P('dp'), may hold values from 0 to 15, all different within a row; in each aligned block of 768 rows (0 to 767, 768 to 1535, ...) at most 480 rows name the same one
- neg_row: int32 [12288, 8], P('dp'), may hold values from 0 to 767
- gain: float32 [4096], replicated, may hold values from 0.5 to 1.5
Outputs:
- grad_queries: bfloat16 [12288, 4096], P('dp', 'group')
- grad_passages: bfloat16 [12288, 4096], P('dp', 'group')
- grad_gain: float32 [4096], replicated
- loss: float32 [], replicated
Inputs may be any that keep to these rules, and one draw needn't show every extreme that they name: `neg_owner`: the 8 owners of one query are distinct; among the 768 queries of one data group no owner is named more than 480 times, and that many in every draw.
All inputs are finite; a program needn't handle non-finite values.
Results may differ from a plain program's by a relative error of at most 0.00305.
The roundings to bfloat16 on the way count: a program that leaves them out, or rounds other values in their place, can miss the bound.
Values may be sent and summed in bfloat16 or wider, within the bound.
A program may use at most 192 MiB of HBM per device.

v0:
```python
import math

import jax
import jax.numpy as jnp
from jax import lax
from jax.sharding import PartitionSpec as P

EPSILON = 1e-06
SOFTNESS_DIVISOR = 0.25


def softmax_rows(scores, near, positive):
    top = jnp.maximum(jnp.max(scores, axis=1), jnp.max(near, axis=1))[:, None]
    total = jnp.sum(jnp.exp(scores - top), axis=1, keepdims=True) + jnp.sum(
        jnp.exp(near - top), axis=1, keepdims=True
    )
    lse = top + jnp.log(total)
    losses = lse[:, 0] - jnp.sum(jnp.where(positive, scores, 0.0), axis=1)
    weights = (jnp.exp(scores - lse) - positive.astype(jnp.float32)).astype(jnp.bfloat16)
    hard_weights = jnp.exp(near - lse).astype(jnp.bfloat16)
    return (weights, hard_weights, losses)


def local(queries, passages, neg_owner, neg_row, gain):
    rows, piece = queries.shape
    negs = neg_owner.shape[1]
    n_data = lax.axis_size("dp")
    n_members = lax.axis_size("group")
    member = lax.axis_index("group")
    hidden_dimension = piece * n_members
    slot_capacity = min(rows, 5 * rows * negs // (4 * n_data))
    multiplier_coefficient = 1.0 / (SOFTNESS_DIVISOR * math.sqrt(hidden_dimension))
    my_gain = lax.dynamic_slice_in_dim(gain, member * piece, piece, 0)
    q_values = queries.astype(jnp.float32)
    p_values = passages.astype(jnp.float32)
    q_square, passage_squares = lax.psum(
        (jnp.sum(q_values * q_values, axis=1), jnp.sum(p_values * p_values, axis=1)), "group"
    )
    q_inverse = lax.rsqrt(q_square / hidden_dimension + EPSILON)[:, None]
    document_reciprocal_norm = lax.rsqrt(passage_squares / hidden_dimension + EPSILON)[:, None]
    q_normed = q_values * q_inverse
    p_normed = p_values * document_reciprocal_norm
    q_emb = (q_normed * my_gain).astype(jnp.bfloat16)
    p_emb = (p_normed * my_gain).astype(jnp.bfloat16)
    owners = neg_owner.reshape(-1)
    owner_hits = (owners[:, None] == jnp.arange(n_data, dtype=jnp.int32)[None, :]).astype(jnp.int32)
    earlier = jnp.cumsum(owner_hits, axis=0) - owner_hits
    slot_of = jnp.sum(earlier * owner_hits, axis=1)
    target = owners * slot_capacity + slot_of
    requested_rows = (
        jnp.zeros((n_data * slot_capacity,), jnp.int32)
        .at[target]
        .set(neg_row.reshape(-1))
        .reshape(n_data, slot_capacity)
    )
    asked = lax.all_to_all(requested_rows, "dp", split_axis=0, concat_axis=0, tiled=True)
    found = jnp.take(p_emb, asked.reshape(-1), axis=0).reshape(asked.shape + (piece,))
    received_block = lax.all_to_all(found, "dp", split_axis=0, concat_axis=0, tiled=True)
    hard = jnp.take(received_block.reshape(-1, piece), target, axis=0).reshape(rows, negs, piece)
    partial_value = (
        jnp.dot(q_emb, p_emb.T, preferred_element_type=jnp.float32) * multiplier_coefficient
    )
    near_part = (
        jnp.einsum("qd,qkd->qk", q_emb, hard, preferred_element_type=jnp.float32)
        * multiplier_coefficient
    )
    share = rows // n_members
    first_row = member * share
    scores, near = lax.psum((partial_value, near_part), "group")
    positive = (
        jnp.arange(rows, dtype=jnp.int32)[None, :] == jnp.arange(rows, dtype=jnp.int32)[:, None]
    )
    weights, hard_weights, losses = softmax_rows(scores, near, positive)
    loss_part = jnp.sum(lax.dynamic_slice_in_dim(losses, first_row, share, 0))
    grad_q = (
        jnp.dot(weights, p_emb, preferred_element_type=jnp.float32)
        + jnp.einsum("qk,qkd->qd", hard_weights, hard, preferred_element_type=jnp.float32)
    ) * multiplier_coefficient
    grad_p = (
        jnp.einsum("qg,qd->gd", weights, q_emb, preferred_element_type=jnp.float32)
        * multiplier_coefficient
    )
    couple_derivatives = (
        (
            (hard_weights.astype(jnp.float32) * multiplier_coefficient)[:, :, None]
            * q_emb.astype(jnp.float32)[:, None, :]
        )
        .astype(jnp.bfloat16)
        .reshape(-1, piece)
    )
    departing_block = (
        jnp.zeros((n_data * slot_capacity, piece), jnp.bfloat16).at[target].set(couple_derivatives)
    )
    returned = lax.all_to_all(
        departing_block.reshape(n_data, slot_capacity, piece),
        "dp",
        split_axis=0,
        concat_axis=0,
        tiled=True,
    )
    select = (asked.reshape(-1)[None, :] == jnp.arange(rows, dtype=jnp.int32)[:, None]).astype(
        jnp.bfloat16
    )
    grad_p = grad_p + jnp.dot(
        select, returned.reshape(-1, piece), preferred_element_type=jnp.float32
    )
    q_inner = grad_q * my_gain
    p_inner = grad_p * my_gain
    q_mean, p_mean = lax.psum(
        (jnp.sum(q_inner * q_normed, axis=1), jnp.sum(p_inner * p_normed, axis=1)), "group"
    )
    grad_queries = (q_inverse * (q_inner - q_normed * (q_mean / hidden_dimension)[:, None])).astype(
        jnp.bfloat16
    )
    grad_passages = (
        document_reciprocal_norm * (p_inner - p_normed * (p_mean / hidden_dimension)[:, None])
    ).astype(jnp.bfloat16)
    gain_part = jnp.sum(grad_q * q_normed, axis=0) + jnp.sum(grad_p * p_normed, axis=0)
    gain_full = lax.dynamic_update_slice_in_dim(
        jnp.zeros((hidden_dimension,), jnp.float32), gain_part, member * piece, 0
    )
    loss_total, gain_total = lax.psum((loss_part, gain_full), ("dp", "group"))
    count = rows * n_data
    return (grad_queries, grad_passages, gain_total / math.sqrt(count), loss_total / count)


def solution(mesh):
    return jax.shard_map(
        local,
        mesh=mesh,
        in_specs=(P("dp", "group"), P("dp", "group"), P("dp", None), P("dp", None), P()),
        out_specs=(P("dp", "group"), P("dp", "group"), P(), P()),
        check_vma=False,
    )
```

profile of v0, /device:TPU:0, one launch (start us, length us, event | category | flops | bytes accessed | tf_op | source)
XLA Modules:
  0.0 2005.0 jit_solution(9707702790398574217)
XLA Ops:
  12.9 1.5 fusion.40
  14.4 8.5 reduce-window.6
  28.9 23.2 %scatter_custom_fusion = s32[7680]{0:T(1024)S(1)} fusion(s32[6144]{0:T(1024)S(1)} %bitcast.52, s32[6144]{0:T(1024)} %reshape.197, s32[]{:T(128)} %constant.28.clone.1), kind=kCustom, calls=%fused_computation.75 | custom fusion | bytes 31232 | tf_op jit(solution)/shard_map/scatter | solution.py:53
  52.8 8.3 all-to-all-start
  61.1 2.6 fusion.34
  64.4 2.5 all-reduce.2
  67.5 6.2 fusion.47
  74.1 29.5 %gather_fusion = bf16[7680,2048]{1,0:T(8,128)(2,1)} fusion(bf16[768,2048]{1,0:T(8,128)(2,1)S(1)} %get-tuple-element.26, s32[8192]{0:T(1024)S(1)} %pad_clamp_fusion), kind=kCustom, calls=%fused_computation | custom fusion | bytes 62945280 | tf_op jit(solution)/shard_map/jit(_take)/gather | solution.py:57
  103.6 21.4 %broadcast_select_fusion = bf16[16,480,2048]{2,1,0:T(8,128)(2,1)} fusion(bf16[16,480,2048]{2,1,0:T(8,128)(2,1)} %bitcast.48, pred[16,480]{1,0:T(8,128)(4,1)S(1)} %compare_and_fusion), kind=kLoop, calls=%fused_computation.7 | loop fusion | flops 15728640 | bytes 62922240 | tf_op jit(solution)/shard_map/jit(_take)/select_n | solution.py:57
  125.1 6.9 all-to-all-start.1
  132.6 5.9 convolution_multiply_fusion
  141.3 7.3 sort
  150.0 11.6 all-reduce.5.cloned.1.call-done
  161.6 1.8 reduce_max.18
  163.4 557.4 %all-to-all-done.1 = bf16[16,480,2048]{2,1,0:T(8,128)(2,1)} async-done(((bf16[16,480,2048]{2,1,0:T(8,128)(2,1)}), bf16[16,480,2048]{2,1,0:T(8,128)(2,1)}, u32[]{:S(2)}, u32[]{:S(2)}) %all-to-all-start.1) | async-done | bytes 31457312 | tf_op jit(solution)/shard_map/all_to_all | solution.py:58
  720.8 143.6 %gather_fusion.1 = bf16[6144,2048]{1,0:T(8,128)(2,1)} fusion(bf16[7680,2048]{1,0:T(8,128)(2,1)} %bitcast.5, s32[6144]{0:T(1024)S(1)} %broadcast_clamp_fusion.1), kind=kCustom, calls=%fused_computation.1 | custom fusion | bytes 50356224 | tf_op jit(solution)/shard_map/jit(_take)/gather | solution.py:59
  864.4 23.0 %fusion.8 = f32[768,1,8]{2,1,0:T(1,128)S(1)} fusion(bf16[6144,2048]{1,0:T(8,128)(2,1)} %gather_fusion.1, pred[768,8]{1,0:T(8,128)(4,1)S(1)} %copy.21, bf16[768,2048,1]{1,0,2:T(8,128)(2,1)} %get-tuple-element.23), kind=kOutput, calls=%fused_computation.14 | convolution fusion | flops 37748736 | bytes 28342272 | tf_op jit(solution)/shard_map/qd,qkd->qk/dot_general | solution.py:64
  888.1 5.0 psum.59
  893.7 2.4 select_reduce_fusion
  898.2 14.1 fusion.1
  912.4 129.8 %scatter_custom_fusion.1 = bf16[7680,2048]{1,0:T(8,128)(2,1)} fusion(s32[6144]{0:T(1024)} %get-tuple-element.4, bf16[6144,2048]{1,0:T(8,128)(2,1)} %fusion.1, s32[6144]{0:T(1024)} %broadcast_clamp_fusion, bf16[]{:T(256)} %constant.72.clone.1), kind=kCustom, calls=%fused_computation.8 | custom fusion | bytes 31457792 | tf_op jit(solution)/shard_map/scatter | solution.py:92
  1042.2 141.7 %all-to-all-start.2 = ((bf16[16,480,2048]{2,1,0:T(8,128)(2,1)}), bf16[16,480,2048]{2,1,0:T(8,128)(2,1)}, u32[]{:S(2)}, u32[]{:S(2)}) async-start(bf16[16,480,2048]{2,1,0:T(8,128)(2,1)} %bitcast.47), calls=%async_computation.2 | async-start | bytes 62914560 | tf_op jit(solution)/shard_map/all_to_all | solution.py:94
  1184.7 14.1 fusion.7
  1198.9 9.2 fusion.26
  1208.0 565.2 %all-to-all-done.2 = bf16[16,480,2048]{2,1,0:T(8,128)(2,1)} async-done(((bf16[16,480,2048]{2,1,0:T(8,128)(2,1)}), bf16[16,480,2048]{2,1,0:T(8,128)(2,1)}, u32[]{:S(2)}, u32[]{:S(2)}) %all-to-all-start.2) | async-done | bytes 31457312 | tf_op jit(solution)/shard_map/all_to_all | solution.py:94
  1773.3 28.6 %fusion.6 = f32[768,2048]{1,0:T(8,128)S(1)} fusion(bf16[7680,2048]{1,0:T(8,128)(2,1)} %bitcast.13, s32[7680]{0:T(1024)S(1)} %reshape.174), kind=kOutput, calls=%fused_computation.12 | convolution fusion | flops 24165089280 | bytes 37779456 | tf_op jit(solution)/shard_map/dot_general | solution.py:104
  1802.0 7.3 fusion.33
  1809.2 2.5 all-reduce.1
  1811.7 174.4 %all-reduce = (f32[4096]{0:T(1024)S(1)}, f32[]{:T(128)}) all-reduce(f32[4096]{0:T(1024)S(1)} %add_dynamic-update-slice_fusion, f32[]{:T(128)} %dynamic-slice_reduce_fusion), channel_id=1, replica_groups=mesh['dp'=16,'group'=2] {'dp','group'}, use_global_device_ids=true, to_apply=%region_21.22 | all-reduce | flops 4097 | bytes 32776 | tf_op jit(solution)/shard_map/psum | solution.py:122
  1986.7 4.9 fusion.25
  1991.6 1.8 copy-done.7
  1993.4 2.7 fusion.32
  (87 shorter events, 23.5 us)
Async XLA Ops:
  7.2 56.5 %copy-start = (bf16[768,2048]{1,0:T(8,128)(2,1)S(1)}, bf16[768,2048]{1,0:T(8,128)(2,1)}, u32[]{:S(2)}) copy-start(bf16[768,2048]{1,0:T(8,128)(2,1)} %param.5) | copy-start | bytes 9437188
  26.2 40.7 %copy-start.20 = (f32[4096]{0:T(1024)S(1)}, f32[4096]{0:T(1024)}, u32[]{:S(2)}) copy-start(f32[4096]{0:T(1024)} %param.9) | copy-start | bytes 49156
  27.5 0.6 copy-start.10
  28.9 23.9 %copy-start.11 = (s32[6144,1]{0,1:T(1,128)}, s32[6144,1]{0,1:T(1,128)S(1)}, u32[]{:S(2)}) copy-start(s32[6144,1]{0,1:T(1,128)S(1)} %compare_select_fusion.1) | copy-start | bytes 73732
  52.8 21.0 %all-to-all-start = ((s32[16,1,480]{2,1,0:T(1,128)}), s32[16,1,480]{2,1,0:T(1,128)S(1)}, u32[]{:S(2)}, u32[]{:S(2)}) async-start(s32[16,1,480]{2,1,0:T(1,128)} %all_to_all.12), calls=%async_computation | async-start | bytes 65536 | tf_op jit(solution)/shard_map/all_to_all | solution.py:56
  66.9 6.9 copy-start.17
  67.5 65.0 %copy-start.15 = (f32[2048]{0:T(1024)}, f32[2048]{0:T(1024)S(1)}, u32[]{:S(2)}) copy-start(f32[2048]{0:T(1024)S(1)} %get-tuple-element.21) | copy-start | bytes 24580
  73.9 29.8 %copy-start.8 = (s32[16,480]{1,0:T(8,128)}, s32[16,480]{1,0:T(8,128)S(1)}, u32[]{:S(2)}) copy-start(s32[16,480]{1,0:T(8,128)S(1)} %reduce.1) | copy-start | bytes 92164
  125.1 595.8 %all-to-all-start.1 = ((bf16[16,480,2048]{2,1,0:T(8,128)(2,1)}), bf16[16,480,2048]{2,1,0:T(8,128)(2,1)}, u32[]{:S(2)}, u32[]{:S(2)}) async-start(bf16[16,480,2048]{2,1,0:T(8,128)(2,1)} %broadcast_select_fusion), calls=%async_computation.1 | async-start | bytes 62914560 | tf_op jit(solution)/shard_map/all_to_all | solution.py:58
  132.0 29.5 %all-reduce.5.cloned.1.call-start = ((), (), s32[]{:S(2)}) async-start(), calls=%async_computation.3 | async-start | bytes 4718592 | tf_op jit(solution)/shard_map/psum | solution.py:69
  141.3 723.1 %copy-start.13 = (pred[768,8]{1,0:T(8,128)(4,1)}, pred[768,8]{1,0:T(8,128)(4,1)S(1)}, u32[]{:S(2)}) copy-start(pred[768,8]{1,0:T(8,128)(4,1)S(1)} %copy.21) | copy-start | bytes 18436
  1042.2 141.7 %copy-start.9 = (s32[16,480]{1,0:T(8,128)S(1)}, s32[16,480]{1,0:T(8,128)}, u32[]{:S(2)}) copy-start(s32[16,480]{1,0:T(8,128)} %copy-done.8) | copy-start | bytes 92164
  1042.2 142.5 %copy-start.12 = (bf16[768,8,1]{1,0,2:T(8,128)(2,1)S(1)}, bf16[768,8,1]{1,0,2:T(8,128)(2,1)}, u32[]{:S(2)}) copy-start(bf16[768,8,1]{1,0,2:T(8,128)(2,1)} %get-tuple-element.25) | copy-start | bytes 36868
  1042.2 142.5 %copy-start.14 = (pred[768,8]{1,0:T(8,128)(4,1)S(1)}, pred[768,8]{1,0:T(8,128)(4,1)}, u32[]{:S(2)}) copy-start(pred[768,8]{1,0:T(8,128)(4,1)} %copy-done.13) | copy-start | bytes 18436
  1042.2 731.1 %all-to-all-start.2 = ((bf16[16,480,2048]{2,1,0:T(8,128)(2,1)}), bf16[16,480,2048]{2,1,0:T(8,128)(2,1)}, u32[]{:S(2)}, u32[]{:S(2)}) async-start(bf16[16,480,2048]{2,1,0:T(8,128)(2,1)} %bitcast.47), calls=%async_computation.2 | async-start | bytes 62914560 | tf_op jit(solution)/shard_map/all_to_all | solution.py:94
  1184.7 14.2 copy-start.1
  1184.7 14.2 copy-start.5
  1184.7 14.2 copy-start.19
  1773.3 28.6 %copy-start.2 = (bf16[768,2048]{1,0:T(8,128)(2,1)S(1)}, bf16[768,2048]{1,0:T(8,128)(2,1)}, u32[]{:S(2)}) copy-start(bf16[768,2048]{1,0:T(8,128)(2,1)} %param.5) | copy-start | bytes 9437188
  1773.3 28.6 %copy-start.3 = (bf16[768,2048]{1,0:T(8,128)(2,1)S(1)}, bf16[768,2048]{1,0:T(8,128)(2,1)}, u32[]{:S(2)}) copy-start(bf16[768,2048]{1,0:T(8,128)(2,1)} %param.6) | copy-start | bytes 9437188
  1773.3 28.6 %copy-start.6 = (f32[768,768]{1,0:T(8,128)S(1)}, f32[768,768]{1,0:T(8,128)}, u32[]{:S(2)}) copy-start(f32[768,768]{1,0:T(8,128)} %all-reduce.5.cloned.1.call-done) | copy-start | bytes 7077892
  1773.3 28.6 %copy-start.16 = (f32[2048]{0:T(1024)S(1)}, f32[2048]{0:T(1024)}, u32[]{:S(2)}) copy-start(f32[2048]{0:T(1024)} %copy-done.15) | copy-start | bytes 24580
  1773.3 28.6 %copy-start.18 = (f32[768]{0:T(1024)S(1)}, f32[768]{0:T(1024)}, u32[]{:S(2)}) copy-start(f32[768]{0:T(1024)} %copy-done.17) | copy-start | bytes 9220
  1986.7 4.9 copy-start.4
  1986.7 6.7 copy-start.7
Sparse Core Ops, SparseCore 0:
  138.6 22.8 all-reduce.4
where the time goes:
time: 2020 us; the launch traced here: 2000 us
  waiting for transfers between devices  1130 us (56%)
  local copies, waits for them, and re-layouts  339 us (17%)
  blocking collectives  184 us (9%)
  starting transfers between devices  157 us (8%)
  matrix products  88.1 us (4%)
  other arithmetic  85.4 us (4%)
    all_to_all x1, waiting for transfers between devices, local(): lax.all_to_all(departing_block.reshape(n_data, slot_capacity, piece), 'dp...  565 us
    all_to_all x1, waiting for transfers between devices, local(): lax.all_to_all(found, 'dp', split_axis=0, concat_axis=0, tiled=True)  557 us
    psum x1, blocking collectives, local(): loss_total, gain_total = lax.psum((loss_part, gain_full), ('dp', 'group'))  174 us
    gather x1, local copies, waits for them, and re-layouts, local(): jnp.take(received_block.reshape(-1, piece), target, axis=0)  144 us
    all_to_all x1, starting transfers between devices, local(): lax.all_to_all(departing_block.reshape(n_data, slot_capacity, piece), 'dp...  142 us
    scatter x2, local copies, waits for them, and re-layouts, local(): jnp.zeros((n_data * slot_capacity, piece), jnp.bfloat16).at[target]  130 us
  transfers between devices with their start and end apart: 4, of which 3 were waited for; matrix products, arithmetic and copies ran while one was open for 3% of the time, Pallas kernels for 0%

commit v1 on v0

v1 whole, which is shorter than its diff:
```python
import functools
import math

import jax
import jax.numpy as jnp
from jax import lax
from jax.experimental import pallas as pl
from jax.experimental.pallas import tpu as pltpu
from jax.sharding import PartitionSpec as P

EPSILON = 1e-06
SOFTNESS_DIVISOR = 0.25
ROWS_BY_ROWS = (((1,), (1,)), ((), ()))
COLS_BY_COLS = (((0,), (0,)), ((), ()))
VMEM_BYTES = 56 << 20


def column(table, index):
    lane = lax.broadcasted_iota(jnp.int32, table.shape, 1)
    return jnp.sum(jnp.where(lane == index, table, jnp.zeros_like(table)), axis=1, keepdims=True)


def near_kernel(q_ref, p_ref, wanted_ref, near_ref):
    step = pl.program_id(0)

    @pl.when(step == 0)
    def _():
        near_ref[...] = jnp.zeros_like(near_ref)

    products = lax.dot_general(
        q_ref[...], p_ref[0], ROWS_BY_ROWS, preferred_element_type=jnp.float32
    )
    wanted = column(wanted_ref[...], step)
    place = lax.broadcasted_iota(jnp.int32, products.shape, 1)
    picked = jnp.sum(jnp.where(place == wanted, products, 0.0), axis=1, keepdims=True)
    lane = lax.broadcasted_iota(jnp.int32, near_ref.shape, 1)
    near_ref[...] += jnp.where(lane == step, picked, 0.0)


def grad_q_kernel(weights_ref, own_ref, p_ref, wanted_ref, hard_ref, grad_ref):
    step = pl.program_id(0)

    @pl.when(step == 0)
    def _():
        grad_ref[...] = jnp.dot(
            weights_ref[...], own_ref[...], preferred_element_type=jnp.float32
        )

    wanted = column(wanted_ref[...], step)
    hard = column(hard_ref[...], step)
    place = lax.broadcasted_iota(jnp.int32, weights_ref.shape, 1)
    spread = jnp.where(place == wanted, hard, 0.0).astype(jnp.bfloat16)
    grad_ref[...] += jnp.dot(spread, p_ref[0], preferred_element_type=jnp.float32)


def grad_p_kernel(scale, weights_ref, own_ref, q_ref, asked_ref, hard_ref, grad_ref):
    step = pl.program_id(0)

    @pl.when(step == 0)
    def _():
        grad_ref[...] = scale * lax.dot_general(
            weights_ref[...], own_ref[...], COLS_BY_COLS, preferred_element_type=jnp.float32
        )

    hard = column(hard_ref[...], step) * scale
    pairs = (hard * q_ref[0].astype(jnp.float32)).astype(jnp.bfloat16)
    row = lax.broadcasted_iota(jnp.int32, weights_ref.shape, 0)
    select = jnp.where(row == asked_ref[0], 1.0, 0.0).astype(jnp.bfloat16)
    grad_ref[...] += jnp.dot(select, pairs, preferred_element_type=jnp.float32)


def whole(shape):
    return pl.BlockSpec(shape, lambda step: (0,) * len(shape))


def block(shape):
    return pl.BlockSpec((1,) + shape, lambda step: (step, 0, 0))


def call(kernel, blocks, in_specs, out_shape, rows, piece):
    return pl.pallas_call(
        kernel,
        grid=(blocks,),
        in_specs=in_specs,
        out_specs=whole(out_shape),
        out_shape=jax.ShapeDtypeStruct(out_shape, jnp.float32),
        compiler_params=pltpu.CompilerParams(vmem_limit_bytes=VMEM_BYTES),
        cost_estimate=pl.CostEstimate(
            flops=2 * blocks * rows * rows * piece,
            bytes_accessed=2 * blocks * rows * piece,
            transcendentals=0,
        ),
    )


def local(queries, passages, neg_owner, neg_row, gain):
    rows, piece = queries.shape
    n_data = lax.axis_size("dp")
    n_members = lax.axis_size("group")
    member = lax.axis_index("group")
    hidden = piece * n_members
    scale = 1.0 / (SOFTNESS_DIVISOR * math.sqrt(hidden))
    my_gain = lax.dynamic_slice_in_dim(gain, member * piece, piece, 0)
    q_values = queries.astype(jnp.float32)
    p_values = passages.astype(jnp.float32)
    q_square, p_square = lax.psum(
        (jnp.sum(q_values * q_values, axis=1), jnp.sum(p_values * p_values, axis=1)), "group"
    )
    q_inverse = lax.rsqrt(q_square / hidden + EPSILON)[:, None]
    p_inverse = lax.rsqrt(p_square / hidden + EPSILON)[:, None]
    q_emb = (q_values * q_inverse * my_gain).astype(jnp.bfloat16)
    p_emb = (p_values * p_inverse * my_gain).astype(jnp.bfloat16)

    all_p = lax.all_gather(p_emb, "dp", axis=0, tiled=False)
    q_later, _ = lax.optimization_barrier((q_emb, all_p))
    all_q = lax.all_gather(q_later, "dp", axis=0, tiled=False)

    owners = jnp.arange(n_data, dtype=jnp.int32)
    named = neg_owner[:, :, None] == owners[None, None, :]
    wanted = jnp.sum(jnp.where(named, neg_row[:, :, None] + 1, 0), axis=1) - 1

    partial_scores = jnp.dot(q_emb, p_emb.T, preferred_element_type=jnp.float32) * scale
    scores = lax.psum(partial_scores, "group")
    near_part = call(
        near_kernel,
        n_data,
        [whole((rows, piece)), block((rows, piece)), whole((rows, n_data))],
        (rows, n_data),
        rows,
        piece,
    )(q_emb, all_p, wanted)
    near = lax.psum(near_part * scale, "group")
    near = jnp.where(wanted >= 0, near, -jnp.inf)

    positive = (
        jnp.arange(rows, dtype=jnp.int32)[None, :] == jnp.arange(rows, dtype=jnp.int32)[:, None]
    )
    top = jnp.maximum(jnp.max(scores, axis=1), jnp.max(near, axis=1))[:, None]
    total = jnp.sum(jnp.exp(scores - top), axis=1, keepdims=True) + jnp.sum(
        jnp.exp(near - top), axis=1, keepdims=True
    )
    lse = top + jnp.log(total)
    losses = lse[:, 0] - jnp.sum(jnp.where(positive, scores, 0.0), axis=1)
    weights = (jnp.exp(scores - lse) - positive.astype(jnp.float32)).astype(jnp.bfloat16)
    hard = jnp.exp(near - lse).astype(jnp.bfloat16).astype(jnp.float32)

    share = rows // n_members
    loss_part = jnp.sum(lax.dynamic_slice_in_dim(losses, member * share, share, 0))

    sent = jnp.concatenate([wanted.T.astype(jnp.float32), hard.T], axis=1)
    came = lax.all_to_all(sent, "dp", split_axis=0, concat_axis=0, tiled=True)
    asked = came[:, :rows].astype(jnp.int32)[:, None, :]
    asked_hard = came[:, rows:].T

    grad_q = (
        call(
            grad_q_kernel,
            n_data,
            [
                whole((rows, rows)),
                whole((rows, piece)),
                block((rows, piece)),
                whole((rows, n_data)),
                whole((rows, n_data)),
            ],
            (rows, piece),
            rows,
            piece,
        )(weights, p_emb, all_p, wanted, hard)
        * scale
    )
    grad_p = call(
        functools.partial(grad_p_kernel, scale),
        n_data,
        [
            whole((rows, rows)),
            whole((rows, piece)),
            block((rows, piece)),
            block((1, rows)),
            whole((rows, n_data)),
        ],
        (rows, piece),
        rows,
        piece,
    )(weights, q_emb, all_q, asked, asked_hard)

    q_normed = q_values * q_inverse
    p_normed = p_values * p_inverse
    q_inner = grad_q * my_gain
    p_inner = grad_p * my_gain
    q_mean, p_mean = lax.psum(
        (jnp.sum(q_inner * q_normed, axis=1), jnp.sum(p_inner * p_normed, axis=1)), "group"
    )
    grad_queries = (q_inverse * (q_inner - q_normed * (q_mean / hidden)[:, None])).astype(
        jnp.bfloat16
    )
    grad_passages = (p_inverse * (p_inner - p_normed * (p_mean / hidden)[:, None])).astype(
        jnp.bfloat16
    )
    gain_part = jnp.sum(grad_q * q_normed, axis=0) + jnp.sum(grad_p * p_normed, axis=0)
    gain_full = lax.dynamic_update_slice_in_dim(
        jnp.zeros((hidden,), jnp.float32), gain_part, member * piece, 0
    )
    loss_total, gain_total = lax.psum((loss_part, gain_full), ("dp", "group"))
    count = rows * n_data
    return (grad_queries, grad_passages, gain_total / math.sqrt(count), loss_total / count)


def solution(mesh):
    return jax.shard_map(
        local,
        mesh=mesh,
        in_specs=(P("dp", "group"), P("dp", "group"), P("dp", None), P("dp", None), P()),
        out_specs=(P("dp", "group"), P("dp", "group"), P(), P()),
        check_vma=False,
    )
```

time: 2020 us -> 1170 us (0.58)
  local copies, waits for them, and re-layouts: 339 us -> 7.91 us
  waiting for transfers between devices: 1130 us -> 878 us
  Pallas kernels: 0 us -> 157 us
  starting transfers between devices: 157 us -> 3.84 us
  blocking collectives: 184 us -> 49.6 us
  matrix products: 88.1 us -> 6.9 us
  other arithmetic: 85.4 us -> 45.6 us
    all_to_all x3 -> x1, waiting for transfers between devices: 1120 us -> 0.01 us  [local(): came = lax.all_to_all(sent, 'dp', split_axis=0, concat_axis=0, tiled=True)]
    all_gather x0 -> x2, waiting for transfers between devices: none -> 878 us  [the longest x1 505 us: local(): all_p = lax.all_gather(p_emb, 'dp', axis=0, tiled=False)]
    gather x2 -> x0, local copies, waits for them, and re-layouts: 173 us -> none  [the longest x1 144 us: local(): jnp.take(received_block.reshape(-1, piece), target, axis=0)]
    pallas_call x0 -> x3, Pallas kernels: none -> 157 us  [the longest x1 55.4 us: local(): call(functools.partial(grad_p_kernel, scale), n_data, [whole((rows, rows)...]
    all_to_all x3 -> x1, starting transfers between devices: 157 us -> 3.72 us  [local(): came = lax.all_to_all(sent, 'dp', split_axis=0, concat_axis=0, tiled=True)]
    scatter x3 -> x0, local copies, waits for them, and re-layouts: 153 us -> none  [the longest x2 130 us: local(): jnp.zeros((n_data * slot_capacity, piece), jnp.bfloat16).at[target]]
    psum x1, blocking collectives: 174 us -> 38.8 us  [local(): loss_total, gain_total = lax.psum((loss_part, gain_full), ('dp', 'group'))]
    dot_general x6 -> x1, matrix products: 88.1 us -> 6.9 us  [local(): jnp.dot(q_emb, p_emb.T, preferred_element_type=jnp.float32) * scale]
  transfers between devices with their start and end apart: 4 -> 4, of which waited for: 3 -> 2; matrix products, arithmetic and copies ran while one was open for 3% -> 3% of each run, Pallas kernels for 0% -> 9%
where the time goes in v1:
time: 1170 us
  waiting for transfers between devices  878 us (75%)
  Pallas kernels  157 us (13%)
  blocking collectives  49.6 us (4%)
  other arithmetic  45.6 us (4%)
  between operations  17.5 us (1%)
    all_gather x1, waiting for transfers between devices, local(): all_p = lax.all_gather(p_emb, 'dp', axis=0, tiled=False)  505 us
    all_gather x1, waiting for transfers between devices, local(): all_q = lax.all_gather(q_later, 'dp', axis=0, tiled=False)  373 us
    pallas_call x1, Pallas kernels, local(): call(functools.partial(grad_p_kernel, scale), n_data, [whole((rows, rows)...  55.4 us
    pallas_call x1, Pallas kernels, local(): call(grad_q_kernel, n_data, [whole((rows, rows)), whole((rows, piece)), b...  53.9 us
    pallas_call x1, Pallas kernels, local(): call(near_kernel, n_data, [whole((rows, piece)), block((rows, piece)), wh...  47.9 us
    psum x1, blocking collectives, local(): loss_total, gain_total = lax.psum((loss_part, gain_full), ('dp', 'group'))  38.8 us
  transfers between devices with their start and end apart: 4, of which 2 were waited for; matrix products, arithmetic and copies ran while one was open for 3% of the time, Pallas kernels for 9%

profile of v1, /device:TPU:0, one launch (start us, length us, event | category | flops | bytes accessed | tf_op | source)
XLA Modules:
  0.0 1166.3 jit_solution(11954113344419428020)
XLA Ops:
  8.1 2.7 fusion.14
  10.8 2.6 fusion.21
  13.4 2.6 all-reduce.2
  16.1 4.9 fusion.15
  21.1 6.9 convolution_multiply_fusion
  28.0 505.0 %all-gather.5.cloned.1.call-done = bf16[12288,2048]{1,0:T(8,128)(2,1)} async-done(((bf16[768,2048]{1,0:T(8,128)(2,1)}), bf16[12288,2048]{1,0:T(8,128)(2,1)}) %all-gather.5.cloned.1.call-update) | async-done | bytes 50331664 | tf_op jit(solution)/shard_map/all_gather | solution.py:114
  533.8 1.0 copy.23
  534.7 0.9 convert_bitcast_fusion
  535.7 1.8 copy.25
  537.4 2.4 reduce_max.18
  539.9 47.9 %shard_map.84 = f32[768,16]{1,0:T(8,128)} custom-call(bf16[768,2048]{1,0:T(8,128)(2,1)} %get-tuple-element.5.q_ref.own_ref, bf16[16,768,2048]{2,1,0:T(8,128)(2,1)} %bitcast.15, s32[768,16]{1,0:T(8,128)} %get-tuple-element.29.wanted_ref), custom_call_target="tpu_custom_call" | custom-call | flops 38654705664 | bytes 50331648 | tf_op jit(solution)/shard_map/pallas_call | solution.py:124
  587.7 1.8 broadcast_multiply_fusion
  589.6 5.7 psum.59
  595.2 1.2 fusion.26
  597.4 2.4 select_reduce_fusion
  600.4 0.9 fusion.24
  602.1 0.8 pad_maximum_fusion
  603.7 3.7 all-to-all-start
  607.4 3.1 subtract_convert_fusion.weights_ref
  610.4 53.9 %shard_map.85 = f32[768,2048]{1,0:T(8,128)} custom-call(bf16[768,768]{1,0:T(8,128)(2,1)} %subtract_convert_fusion.weights_ref, bf16[768,2048]{1,0:T(8,128)(2,1)} %get-tuple-element.30.own_ref, bf16[16,768,2048]{2,1,0:T(8,128)(2,1)} %bitcast.16, s32[768,16]{1,0:T(8,128)} %get-tuple-element.29.wanted_ref, f32[768,16]{1,0:T(8,128)} %get-tuple-element.27.hard_ref), custom_call_target="tpu_custom_call" | custom-call | flops 38654705664 | bytes 50331648 | tf_op jit(solution)/shard_map/pallas_call | solution.py:156
  664.4 4.8 fusion.13
  669.8 1.2 copy.27
  671.0 1.9 slice_bitcast_fusion
  672.9 0.8 copy.28.asked_ref
  673.7 372.7 %all-gather.7.cloned.1.call-done = bf16[12288,2048]{1,0:T(8,128)(2,1)} async-done(((bf16[768,2048]{1,0:T(8,128)(2,1)}), bf16[12288,2048]{1,0:T(8,128)(2,1)}) %all-gather.7.cloned.1.call-update) | async-done | bytes 50331664 | tf_op jit(solution)/shard_map/all_gather | solution.py:116
  1046.3 55.4 %shard_map.86 = f32[768,2048]{1,0:T(8,128)} custom-call(bf16[768,768]{1,0:T(8,128)(2,1)} %subtract_convert_fusion.weights_ref, bf16[768,2048]{1,0:T(8,128)(2,1)} %get-tuple-element.5.q_ref.own_ref, bf16[16,768,2048]{2,1,0:T(8,128)(2,1)} %bitcast.14, s32[16,1,768]{2,1,0:T(1,128)} %copy.28.asked_ref, f32[768,16]{1,0:T(8,128)} %get-tuple-element.24.hard_ref), custom_call_target="tpu_custom_call" | custom-call | flops 38654705664 | bytes 50331648 | tf_op jit(solution)/shard_map/pallas_call | solution.py:172
  1101.8 3.8 fusion.20
  1105.6 2.5 all-reduce.1
  1108.1 5.0 fusion.12
  1113.1 1.8 copy-done.3
  1114.9 2.7 fusion.19
  1117.6 38.8 %all-reduce = (f32[4096]{0:T(1024)S(1)}, f32[]{:T(128)}) all-reduce(f32[4096]{0:T(1024)S(1)} %add_dynamic-update-slice_fusion, f32[]{:T(128)} %dynamic-slice_reduce_fusion), channel_id=1, replica_groups=mesh['dp'=16,'group'=2] {'dp','group'}, use_global_device_ids=true, to_apply=%region_17.18 | all-reduce | flops 4097 | bytes 32776 | tf_op jit(solution)/shard_map/psum | solution.py:204
  (54 shorter events, 5.3 us)
Async XLA Ops:
  8.0 8.0 copy-start
  8.0 8.0 copy-start.15
  8.0 525.0 %all-gather.5.cloned.1.call-start = ((), (), s32[]{:S(2)}) async-start(), calls=%async_computation.2 | async-start | bytes 53477376 | tf_op jit(solution)/shard_map/all_gather | solution.py:114
  16.0 5.0 copy-start.4
  16.0 4.9 copy-start.6
  21.0 516.5 %all-reduce.5.cloned.1.call-start = ((), (), s32[]{:S(2)}) async-start(), calls=%async_computation.1 | async-start | bytes 4718592 | tf_op jit(solution)/shard_map/psum | solution.py:123
  21.0 512.1 %copy-start.11 = (s32[768,8]{0,1:T(8,128)S(1)}, s32[768,8]{0,1:T(8,128)}, u32[]{:S(2)}) copy-start(s32[768,8]{0,1:T(8,128)} %param.8) | copy-start | bytes 73732
  21.0 512.1 %copy-start.12 = (s32[768,8]{0,1:T(8,128)S(1)}, s32[768,8]{0,1:T(8,128)}, u32[]{:S(2)}) copy-start(s32[768,8]{0,1:T(8,128)} %param.7) | copy-start | bytes 73732
  28.0 1018.3 %all-gather.7.cloned.1.call-start = ((), (), s32[]{:S(2)}) async-start(), calls=%async_computation.3 | async-start | bytes 53477376 | tf_op jit(solution)/shard_map/all_gather | solution.py:116
  600.4 0.9 copy-start.9
  603.7 66.2 %all-to-all-start = ((f32[16,1,1536]{2,1,0:T(1,128)}), f32[16,1,1536]{2,1,0:T(1,128)S(1)}, u32[]{:S(2)}, u32[]{:S(2)}) async-start(f32[16,1,1536]{2,1,0:T(1,128)} %all_to_all.8), calls=%async_computation | async-start | bytes 196608 | tf_op jit(solution)/shard_map/all_to_all | solution.py:151
  610.4 53.9 %copy-start.7 = (f32[768]{0:T(1024)S(1)}, f32[768]{0:T(1024)}, u32[]{:S(2)}) copy-start(f32[768]{0:T(1024)} %copy-done.6) | copy-start | bytes 9220
  664.4 4.8 copy-start.14
  1046.3 55.4 %copy-start.1 = (bf16[768,2048]{1,0:T(8,128)(2,1)S(1)}, bf16[768,2048]{1,0:T(8,128)(2,1)}, u32[]{:S(2)}) copy-start(bf16[768,2048]{1,0:T(8,128)(2,1)} %param.6) | copy-start | bytes 9437188
  1046.3 55.4 %copy-start.5 = (f32[768]{0:T(1024)S(1)}, f32[768]{0:T(1024)}, u32[]{:S(2)}) copy-start(f32[768]{0:T(1024)} %copy-done.4) | copy-start | bytes 9220
  1101.7 3.9 copy-start.13
  1101.7 6.4 copy-start.8
  1108.1 5.0 copy-start.2
  1108.1 6.7 copy-start.3
  1114.9 2.8 copy-start.10
Sparse Core Ops, SparseCore 0:
  21.1 511.9 all-gather.4
  536.8 509.4 all-gather.6
Sparse Core Ops, SparseCore 1:
  28.1 23.9 all-reduce.4

commit v2 on v1

v2 whole, which is shorter than its diff:
```python
import functools
import math

import jax
import jax.numpy as jnp
from jax import lax
from jax.experimental import pallas as pl
from jax.experimental.pallas import tpu as pltpu
from jax.sharding import PartitionSpec as P

EPSILON = 1e-06
SOFTNESS_DIVISOR = 0.25
ROWS_BY_ROWS = (((1,), (1,)), ((), ()))
COLS_BY_COLS = (((0,), (0,)), ((), ()))
VMEM_BYTES = 56 << 20


def column(table, index):
    lane = lax.broadcasted_iota(jnp.int32, table.shape, 1)
    return jnp.sum(jnp.where(lane == index, table, jnp.zeros_like(table)), axis=1, keepdims=True)


def near_kernel(q_ref, p_ref, wanted_ref, near_ref):
    step = pl.program_id(1)

    @pl.when(step == 0)
    def _():
        near_ref[...] = jnp.zeros_like(near_ref)

    products = lax.dot_general(
        q_ref[0], p_ref[0], ROWS_BY_ROWS, preferred_element_type=jnp.float32
    )
    wanted = column(wanted_ref[0], step)
    place = lax.broadcasted_iota(jnp.int32, products.shape, 1)
    picked = jnp.sum(jnp.where(place == wanted, products, 0.0), axis=1, keepdims=True)
    lane = lax.broadcasted_iota(jnp.int32, near_ref.shape[1:], 1)
    near_ref[0] += jnp.where(lane == step, picked, 0.0)


def add_q_term(p_ref, wanted_ref, hard_ref, total_ref, step):
    wanted = column(wanted_ref[...], step)
    hard = column(hard_ref[...], step)
    rows = wanted.shape[0]
    place = lax.broadcasted_iota(jnp.int32, (rows, rows), 1)
    spread = jnp.where(place == wanted, hard, 0.0).astype(jnp.bfloat16)
    total_ref[...] += jnp.dot(spread, p_ref[0], preferred_element_type=jnp.float32)


def add_p_term(scale, q_ref, asked_ref, hard_ref, total_ref, step):
    hard = column(hard_ref[...], step) * scale
    pairs = (hard * q_ref[0].astype(jnp.float32)).astype(jnp.bfloat16)
    rows = pairs.shape[0]
    row = lax.broadcasted_iota(jnp.int32, (rows, rows), 0)
    select = jnp.where(row == asked_ref[0], 1.0, 0.0).astype(jnp.bfloat16)
    total_ref[...] += jnp.dot(select, pairs, preferred_element_type=jnp.float32)


def own_q_kernel(weights_ref, own_ref, p_ref, wanted_ref, hard_ref, grad_ref):
    step = pl.program_id(0)

    @pl.when(step == 0)
    def _():
        grad_ref[...] = jnp.dot(
            weights_ref[...], own_ref[...], preferred_element_type=jnp.float32
        )

    add_q_term(p_ref, wanted_ref, hard_ref, grad_ref, step)


def own_p_kernel(scale, weights_ref, own_ref, q_ref, asked_ref, hard_ref, grad_ref):
    step = pl.program_id(0)

    @pl.when(step == 0)
    def _():
        grad_ref[...] = scale * lax.dot_general(
            weights_ref[...], own_ref[...], COLS_BY_COLS, preferred_element_type=jnp.float32
        )

    add_p_term(scale, q_ref, asked_ref, hard_ref, grad_ref, step)


def sent_q_kernel(p_ref, wanted_ref, hard_ref, grad_ref, total_ref):
    step = pl.program_id(0)

    @pl.when(step == 0)
    def _():
        total_ref[...] = jnp.zeros_like(total_ref)

    add_q_term(p_ref, wanted_ref, hard_ref, total_ref, step)

    @pl.when(step == pl.num_programs(0) - 1)
    def _():
        grad_ref[...] = total_ref[...].astype(grad_ref.dtype)


def sent_p_kernel(scale, q_ref, asked_ref, hard_ref, grad_ref, total_ref):
    step = pl.program_id(0)

    @pl.when(step == 0)
    def _():
        total_ref[...] = jnp.zeros_like(total_ref)

    add_p_term(scale, q_ref, asked_ref, hard_ref, total_ref, step)

    @pl.when(step == pl.num_programs(0) - 1)
    def _():
        grad_ref[...] = total_ref[...].astype(grad_ref.dtype)


def whole(shape):
    return pl.BlockSpec(shape, lambda step: (0,) * len(shape))


def block(shape):
    return pl.BlockSpec((1,) + shape, lambda step: (step, 0, 0))


def params():
    return pltpu.CompilerParams(vmem_limit_bytes=VMEM_BYTES)


def cost(blocks, rows, piece):
    return pl.CostEstimate(
        flops=2 * blocks * rows * rows * piece,
        bytes_accessed=2 * blocks * rows * piece,
        transcendentals=0,
    )


def call(kernel, blocks, in_specs, dtype, rows, piece):
    scratch = [] if dtype == jnp.float32 else [pltpu.VMEM((rows, piece), jnp.float32)]
    return pl.pallas_call(
        kernel,
        grid=(blocks,),
        in_specs=in_specs,
        out_specs=whole((rows, piece)),
        out_shape=jax.ShapeDtypeStruct((rows, piece), dtype),
        scratch_shapes=scratch,
        compiler_params=params(),
        cost_estimate=cost(blocks, rows, piece),
    )


def local(queries, passages, neg_owner, neg_row, gain):
    rows, piece = queries.shape
    n_data = lax.axis_size("dp")
    n_members = lax.axis_size("group")
    member = lax.axis_index("group")
    hidden = piece * n_members
    scale = 1.0 / (SOFTNESS_DIVISOR * math.sqrt(hidden))
    my_gain = lax.dynamic_slice_in_dim(gain, member * piece, piece, 0)
    q_values = queries.astype(jnp.float32)
    p_values = passages.astype(jnp.float32)
    q_square, p_square = lax.psum(
        (jnp.sum(q_values * q_values, axis=1), jnp.sum(p_values * p_values, axis=1)), "group"
    )
    q_inverse = lax.rsqrt(q_square / hidden + EPSILON)[:, None]
    p_inverse = lax.rsqrt(p_square / hidden + EPSILON)[:, None]
    q_emb = (q_values * q_inverse * my_gain).astype(jnp.bfloat16)
    p_emb = (p_values * p_inverse * my_gain).astype(jnp.bfloat16)

    lines = 2 ** (int(math.log2(n_data)) // 2)
    plane = n_data // lines
    line_groups = [[a * plane + b for a in range(lines)] for b in range(plane)]
    plane_groups = [[a * plane + b for b in range(plane)] for a in range(lines)]
    here = lax.rem(lax.axis_index("dp"), plane)

    def exchange(table, groups):
        flat = table.reshape(table.shape[0], -1)
        came = lax.all_to_all(
            flat, "dp", split_axis=0, concat_axis=0, axis_index_groups=groups, tiled=True
        )
        return came.reshape(table.shape)

    line_q = lax.all_gather(q_emb, "dp", axis_index_groups=line_groups)
    plane_p = lax.all_gather(p_emb, "dp", axis_index_groups=plane_groups)
    p_later, _ = lax.optimization_barrier((p_emb, line_q))
    line_p = lax.all_gather(p_later, "dp", axis_index_groups=line_groups)

    owners = jnp.arange(n_data, dtype=jnp.int32)[:, None, None]
    named = neg_owner.T[None] == owners
    wanted = (jnp.sum(jnp.where(named, neg_row.T[None] + 1, 0), axis=1) - 1).reshape(
        lines, plane, rows
    )
    line_wanted = exchange(wanted, line_groups)
    plane_wanted = exchange(wanted.transpose(1, 0, 2), plane_groups).transpose(0, 2, 1)

    partial_scores = jnp.dot(q_emb, p_emb.T, preferred_element_type=jnp.float32) * scale
    scores = lax.psum(partial_scores, "group")
    near_part = pl.pallas_call(
        near_kernel,
        grid=(lines, plane),
        in_specs=[
            pl.BlockSpec((1, rows, piece), lambda a, b: (a, 0, 0)),
            pl.BlockSpec((1, rows, piece), lambda a, b: (b, 0, 0)),
            pl.BlockSpec((1, rows, plane), lambda a, b: (a, 0, 0)),
        ],
        out_specs=pl.BlockSpec((1, rows, plane), lambda a, b: (a, 0, 0)),
        out_shape=jax.ShapeDtypeStruct((lines, rows, plane), jnp.float32),
        compiler_params=params(),
        cost_estimate=cost(n_data, rows, piece),
    )(line_q, plane_p, line_wanted.transpose(0, 2, 1))
    line_near = lax.psum(near_part.transpose(0, 2, 1) * scale, "group")
    near = jnp.where(wanted >= 0, exchange(line_near, line_groups), -jnp.inf)
    near = near.reshape(n_data, rows)

    positive = (
        jnp.arange(rows, dtype=jnp.int32)[None, :] == jnp.arange(rows, dtype=jnp.int32)[:, None]
    )
    top = jnp.maximum(jnp.max(scores, axis=1), jnp.max(near, axis=0))
    total = jnp.sum(jnp.exp(scores - top[:, None]), axis=1) + jnp.sum(
        jnp.exp(near - top[None, :]), axis=0
    )
    lse = top + jnp.log(total)
    losses = lse - jnp.sum(jnp.where(positive, scores, 0.0), axis=1)
    weights = (jnp.exp(scores - lse[:, None]) - positive.astype(jnp.float32)).astype(jnp.bfloat16)
    hard = jnp.exp(near - lse[None, :]).astype(jnp.bfloat16).astype(jnp.float32)
    hard = hard.reshape(lines, plane, rows)

    share = rows // n_members
    loss_part = jnp.sum(lax.dynamic_slice_in_dim(losses, member * share, share, 0))

    line_hard = exchange(hard, line_groups)
    plane_hard = exchange(hard.transpose(1, 0, 2), plane_groups).transpose(0, 2, 1)

    def partner_of(shift):
        return [
            (a * plane + b, a * plane + (b ^ shift)) for a in range(lines) for b in range(plane)
        ]

    def p_tables(target):
        asked = lax.dynamic_index_in_dim(line_wanted, target, 1, keepdims=True)
        asked_hard = lax.dynamic_index_in_dim(line_hard, target, 1, keepdims=False).T
        return asked, asked_hard

    def q_tables(target):
        return (
            lax.dynamic_index_in_dim(plane_wanted, target, 0, keepdims=False),
            lax.dynamic_index_in_dim(plane_hard, target, 0, keepdims=False),
        )

    p_specs = [block((rows, piece)), block((1, rows)), whole((rows, lines))]
    q_specs = [block((rows, piece)), whole((rows, lines)), whole((rows, lines))]
    batch_specs = [whole((rows, rows)), whole((rows, piece))]
    size = (rows, piece)
    shifts = range(plane - 1, 0, -1)

    p_parts = []
    for shift in shifts:
        part = call(
            functools.partial(sent_p_kernel, scale), lines, p_specs, jnp.bfloat16, *size
        )(line_q, *p_tables(here ^ shift))
        p_parts.append(lax.ppermute(part, "dp", partner_of(shift)))
    grad_p = call(
        functools.partial(own_p_kernel, scale), lines, batch_specs + p_specs, jnp.float32, *size
    )(weights, q_emb, line_q, *p_tables(here))
    q_parts = []
    for shift in shifts:
        part = call(sent_q_kernel, lines, q_specs, jnp.bfloat16, *size)(
            line_p, *q_tables(here ^ shift)
        )
        q_parts.append(lax.ppermute(part, "dp", partner_of(shift)))
    grad_q = call(own_q_kernel, lines, batch_specs + q_specs, jnp.float32, *size)(
        weights, p_emb, line_p, *q_tables(here)
    )
    for part in p_parts:
        grad_p = grad_p + part.astype(jnp.float32)
    for part in q_parts:
        grad_q = grad_q + part.astype(jnp.float32)
    grad_q = grad_q * scale

    q_normed = q_values * q_inverse
    p_normed = p_values * p_inverse
    q_inner = grad_q * my_gain
    p_inner = grad_p * my_gain
    q_mean, p_mean = lax.psum(
        (jnp.sum(q_inner * q_normed, axis=1), jnp.sum(p_inner * p_normed, axis=1)), "group"
    )
    grad_queries = (q_inverse * (q_inner - q_normed * (q_mean / hidden)[:, None])).astype(
        jnp.bfloat16
    )
    grad_passages = (p_inverse * (p_inner - p_normed * (p_mean / hidden)[:, None])).astype(
        jnp.bfloat16
    )
    gain_part = jnp.sum(grad_q * q_normed, axis=0) + jnp.sum(grad_p * p_normed, axis=0)
    gain_full = lax.dynamic_update_slice_in_dim(
        jnp.zeros((hidden,), jnp.float32), gain_part, member * piece, 0
    )
    loss_total, gain_total = lax.psum((loss_part, gain_full), ("dp", "group"))
    count = rows * n_data
    return (grad_queries, grad_passages, gain_total / math.sqrt(count), loss_total / count)


def solution(mesh):
    return jax.shard_map(
        local,
        mesh=mesh,
        in_specs=(P("dp", "group"), P("dp", "group"), P("dp", None), P("dp", None), P()),
        out_specs=(P("dp", "group"), P("dp", "group"), P(), P()),
        check_vma=False,
    )
```

time: 1170 us -> 832 us (0.71)
  waiting for transfers between devices: 878 us -> 473 us
  Pallas kernels: 157 us -> 185 us
  starting transfers between devices: 3.84 us -> 25.5 us
  local copies, waits for them, and re-layouts: 7.91 us -> 21.7 us
    all_gather x2 -> x3, waiting for transfers between devices: 878 us -> 380 us  [the longest x1 213 us: local(): line_q = lax.all_gather(q_emb, 'dp', axis_index_groups=line_groups)]
    ppermute x0 -> x6, waiting for transfers between devices: none -> 64 us  [the longest x3 64 us: local(): q_parts.append(lax.ppermute(part, 'dp', partner_of(shift)))]
    all_to_all x1 -> x5, waiting for transfers between devices: 0.01 us -> 28.8 us  [exchange(): lax.all_to_all(flat, 'dp', split_axis=0, concat_axis=0, axis_index_groups...]
    pallas_call x3 -> x9, Pallas kernels: 157 us -> 185 us  [the longest x1 49.5 us: local(): pl.pallas_call(near_kernel, grid=(lines, plane), in_specs=[pl.BlockSpec((...]
    all_to_all x1 -> x5, starting transfers between devices: 3.72 us -> 18.4 us  [exchange(): lax.all_to_all(flat, 'dp', split_axis=0, concat_axis=0, axis_index_groups...]
  transfers between devices with their start and end apart: 4 -> 15, of which waited for: 2 -> 11; matrix products, arithmetic and copies ran while one was open for 3% -> 6% of each run, Pallas kernels for 9% -> 23%
where the time goes in v2:
time: 832 us; the launch traced here: 823 us
  waiting for transfers between devices  473 us (57%)
  Pallas kernels  185 us (22%)
  blocking collectives  48.2 us (6%)
  other arithmetic  44.2 us (5%)
  starting transfers between devices  25.5 us (3%)
  local copies, waits for them, and re-layouts  21.7 us (3%)
  between operations  17.7 us (2%)
    all_gather x1, waiting for transfers between devices, local(): line_q = lax.all_gather(q_emb, 'dp', axis_index_groups=line_groups)  213 us
    all_gather x1, waiting for transfers between devices, local(): plane_p = lax.all_gather(p_emb, 'dp', axis_index_groups=plane_groups)  103 us
    ppermute x3, waiting for transfers between devices, local(): q_parts.append(lax.ppermute(part, 'dp', partner_of(shift)))  64 us
    all_gather x1, waiting for transfers between devices, local(): line_p = lax.all_gather(p_later, 'dp', axis_index_groups=line_groups)  63.4 us
    pallas_call x1, Pallas kernels, local(): pl.pallas_call(near_kernel, grid=(lines, plane), in_specs=[pl.BlockSpec((...  49.5 us
    pallas_call x3, Pallas kernels, local(): call(functools.partial(sent_p_kernel, scale), lines, p_specs, jnp.bfloat1...  47.9 us
    pallas_call x3, Pallas kernels, local(): call(sent_q_kernel, lines, q_specs, jnp.bfloat16, *size)  47.5 us
    psum x1, blocking collectives, local(): loss_total, gain_total = lax.psum((loss_part, gain_full), ('dp', 'group'))  39.6 us
  transfers between devices with their start and end apart: 15, of which 11 were waited for; matrix products, arithmetic and copies ran while one was open for 6% of the time, Pallas kernels for 23%

profile of v2, /device:TPU:0, one launch (start us, length us, event | category | flops | bytes accessed | tf_op | source)
XLA Modules:
  0.0 822.8 jit_solution(13457149282313619584)
XLA Ops:
  14.2 4.9 fusion.8
  19.9 6.9 convolution_multiply_fusion
  26.9 213.2 %all-gather.7.cloned.1.call-done = bf16[3072,2048]{1,0:T(8,128)(2,1)} async-done(((bf16[768,2048]{1,0:T(8,128)(2,1)}), bf16[3072,2048]{1,0:T(8,128)(2,1)}) %all-gather.7.cloned.1.call-update) | async-done | bytes 12582928 | tf_op jit(solution)/shard_map/all_gather | solution.py:175
  240.9 3.7 all-to-all-start.2
  245.3 4.1 all-to-all-done.2
  249.4 3.3 all-to-all-start
  260.1 103.0 %all-gather.9.cloned.1.call-done = bf16[3072,2048]{1,0:T(8,128)(2,1)} async-done(((bf16[768,2048]{1,0:T(8,128)(2,1)}), bf16[3072,2048]{1,0:T(8,128)(2,1)}) %all-gather.9.cloned.1.call-update) | async-done | bytes 12582928 | tf_op jit(solution)/shard_map/all_gather | solution.py:176
  363.2 49.5 %shard_map.84 = f32[4,768,4]{2,1,0:T(8,128)} custom-call(bf16[4,768,2048]{2,1,0:T(8,128)(2,1)} %bitcast.71, bf16[4,768,2048]{2,1,0:T(8,128)(2,1)} %bitcast.80, s32[4,768,4]{2,1,0:T(8,128)} %copy.77.wanted_ref), custom_call_target="tpu_custom_call" | custom-call | flops 38654705664 | bytes 50331648 | tf_op jit(solution)/shard_map/pallas_call | solution.py:190
  417.3 3.5 psum.59
  421.5 4.7 all-to-all-start.1
  428.8 12.0 %all-to-all-done.1 = f32[4,1,3072]{2,1,0:T(1,128)S(1)} async-done(((f32[4,1,3072]{2,1,0:T(1,128)}), f32[4,1,3072]{2,1,0:T(1,128)S(1)}, u32[]{:S(2)}, u32[]{:S(2)}) %all-to-all-start.1) | async-done | bytes 49184 | tf_op jit(solution)/shard_map/all_to_all | solution.py:170
  444.2 3.3 all-to-all-start.3
  448.9 3.4 all-to-all-done.3
  452.3 3.4 all-to-all-start.4
  458.8 7.8 all-to-all-done.4
  470.8 16.0 %shard_map.90 = bf16[768,2048]{1,0:T(8,128)(2,1)} custom-call(bf16[4,768,2048]{2,1,0:T(8,128)(2,1)} %bitcast.72, s32[4,1,768]{2,1,0:T(1,128)} %get-tuple-element.28.asked_ref, f32[768,4]{1,0:T(8,128)} %get-tuple-element.24.hard_ref), custom_call_target="tpu_custom_call" | custom-call | flops 9663676416 | bytes 12582912 | tf_op jit(solution)/shard_map/pallas_call | solution.py:250
  486.8 16.0 %shard_map.91 = bf16[768,2048]{1,0:T(8,128)(2,1)} custom-call(bf16[4,768,2048]{2,1,0:T(8,128)(2,1)} %bitcast.73, s32[4,1,768]{2,1,0:T(1,128)} %get-tuple-element.30.asked_ref, f32[768,4]{1,0:T(8,128)} %get-tuple-element.26.hard_ref), custom_call_target="tpu_custom_call" | custom-call | flops 9663676416 | bytes 12582912 | tf_op jit(solution)/shard_map/pallas_call | solution.py:250
  502.8 2.9 collective-permute-start.4
  505.7 16.0 %shard_map.92 = bf16[768,2048]{1,0:T(8,128)(2,1)} custom-call(bf16[4,768,2048]{2,1,0:T(8,128)(2,1)} %bitcast.74, s32[4,1,768]{2,1,0:T(1,128)} %get-tuple-element.29.asked_ref, f32[768,4]{1,0:T(8,128)} %get-tuple-element.25.hard_ref), custom_call_target="tpu_custom_call" | custom-call | flops 9663676416 | bytes 12582912 | tf_op jit(solution)/shard_map/pallas_call | solution.py:250
  522.3 63.4 %all-gather.11.cloned.1.call-done = bf16[3072,2048]{1,0:T(8,128)(2,1)} async-done(((bf16[768,2048]{1,0:T(8,128)(2,1)}), bf16[3072,2048]{1,0:T(8,128)(2,1)}) %all-gather.11.cloned.1.call-update) | async-done | bytes 12582928 | tf_op jit(solution)/shard_map/all_gather | solution.py:178
  585.6 15.9 %shard_map.86 = bf16[768,2048]{1,0:T(8,128)(2,1)} custom-call(bf16[4,768,2048]{2,1,0:T(8,128)(2,1)} %bitcast.76, s32[768,4]{1,0:T(8,128)} %bitcast.64, f32[768,4]{1,0:T(8,128)} %bitcast.67), custom_call_target="tpu_custom_call" | custom-call | flops 9663676416 | bytes 12582912 | tf_op jit(solution)/shard_map/pallas_call | solution.py:259
  603.9 15.7 %shard_map.87 = bf16[768,2048]{1,0:T(8,128)(2,1)} custom-call(bf16[4,768,2048]{2,1,0:T(8,128)(2,1)} %bitcast.77, s32[768,4]{1,0:T(8,128)} %bitcast.63, f32[768,4]{1,0:T(8,128)} %bitcast.66), custom_call_target="tpu_custom_call" | custom-call | flops 9663676416 | bytes 12582912 | tf_op jit(solution)/shard_map/pallas_call | solution.py:259
  620.2 15.8 %shard_map.88 = bf16[768,2048]{1,0:T(8,128)(2,1)} custom-call(bf16[4,768,2048]{2,1,0:T(8,128)(2,1)} %bitcast.78, s32[768,4]{1,0:T(8,128)} %bitcast.62, f32[768,4]{1,0:T(8,128)} %bitcast.65), custom_call_target="tpu_custom_call" | custom-call | flops 9663676416 | bytes 12582912 | tf_op jit(solution)/shard_map/pallas_call | solution.py:259
  639.0 20.5 %shard_map.89 = f32[768,2048]{1,0:T(8,128)} custom-call(bf16[768,768]{1,0:T(8,128)(2,1)} %subtract_convert_fusion.weights_ref, bf16[768,2048]{1,0:T(8,128)(2,1)} %get-tuple-element.40.own_ref, bf16[4,768,2048]{2,1,0:T(8,128)(2,1)} %bitcast.75, s32[4,1,768]{2,1,0:T(1,128)} %get-tuple-element.31.asked_ref, f32[768,4]{1,0:T(8,128)} %get-tuple-element.27.hard_ref), custom_call_target="tpu_custom_call" | custom-call | flops 9663676416 | bytes 12582912 | tf_op jit(solution)/shard_map/pallas_call | solution.py:254
  659.5 8.9 %fusion.20 = (f32[2048]{0:T(1024)S(1)}, f32[768]{0:T(1024)S(1)}, f32[768,2048]{1,0:T(8,128)}) fusion(bf16[768,2048]{1,0:T(8,128)(2,1)S(1)} %copy-done, f32[768]{0:T(1024)S(1)} %get-tuple-element.42, f32[2048]{0:T(1024)S(1)} %get-tuple-element.23, bf16[768,2048]{1,0:T(8,128)(2,1)} %collective-permute-done.5, bf16[768,2048]{1,0:T(8,128)(2,1)} %collective-permute-done.4, ...), kind=kLoop, calls=%fused_computation.24 | loop fusion | flops 20444416 | bytes 25188352 | tf_op jit(solution)/shard_map/reduce_sum | solution.py:285
  668.4 20.0 %shard_map.85 = f32[768,2048]{1,0:T(8,128)} custom-call(bf16[768,768]{1,0:T(8,128)(2,1)} %subtract_convert_fusion.weights_ref, bf16[768,2048]{1,0:T(8,128)(2,1)} %get-tuple-element.5.own_ref, bf16[4,768,2048]{2,1,0:T(8,128)(2,1)} %bitcast.79, s32[768,4]{1,0:T(8,128)} %bitcast.61, f32[768,4]{1,0:T(8,128)} %bitcast.68), custom_call_target="tpu_custom_call" | custom-call | flops 9663676416 | bytes 12582912 | tf_op jit(solution)/shard_map/pallas_call | solution.py:263
  688.4 5.6 collective-permute-done
  694.0 58.2 %collective-permute-done.1 = bf16[768,2048]{1,0:T(8,128)(2,1)} collective-permute-done((bf16[768,2048]{1,0:T(8,128)(2,1)}, bf16[768,2048]{1,0:T(8,128)(2,1)}, u32[]{:S(2)}, u32[]{:S(2)}) %collective-permute-start.1) | collective-permute-done | bytes 3145760 | tf_op jit(solution)/shard_map/ppermute | solution.py:262
  752.4 8.8 %fusion.13 = (f32[2048]{0:T(1024)S(1)}, f32[768]{0:T(1024)S(1)}, f32[768,2048]{1,0:T(8,128)}) fusion(bf16[768,2048]{1,0:T(8,128)(2,1)S(1)} %copy-done.1, f32[768]{0:T(1024)S(1)} %get-tuple-element.43, f32[2048]{0:T(1024)S(1)} %get-tuple-element.22, bf16[768,2048]{1,0:T(8,128)(2,1)} %collective-permute-done.2, bf16[768,2048]{1,0:T(8,128)(2,1)} %collective-permute-done.1, ...), kind=kLoop, calls=%fused_computation.17 | loop fusion | flops 22017280 | bytes 25188352 | tf_op jit(solution)/shard_map/reduce_sum | solution.py:285
  761.3 39.6 %all-reduce = (f32[4096]{0:T(1024)S(1)}, f32[]{:T(128)}) all-reduce(f32[4096]{0:T(1024)S(1)} %add_dynamic-update-slice_fusion, f32[]{:T(128)} %dynamic-slice_reduce_fusion), channel_id=1, replica_groups=mesh['dp'=16,'group'=2] {'dp','group'}, use_global_device_ids=true, to_apply=%region_17.18 | all-reduce | flops 4097 | bytes 32776 | tf_op jit(solution)/shard_map/psum | solution.py:289
  804.6 4.9 fusion.19
  811.4 2.8 fusion.12
  (94 shorter events, 47.4 us)
Async XLA Ops:
  8.0 2.8 copy-start
  8.0 232.0 %all-gather.7.cloned.1.call-start = ((), (), s32[]{:S(2)}) async-start(), calls=%async_computation.6 | async-start | bytes 15728640 | tf_op jit(solution)/shard_map/all_gather | solution.py:175
  8.1 3.5 copy-start.7
  19.1 344.1 %all-gather.9.cloned.1.call-start = ((), (), s32[]{:S(2)}) async-start(), calls=%async_computation.7 | async-start | bytes 15728640 | tf_op jit(solution)/shard_map/all_gather | solution.py:176
  19.8 407.1 %all-reduce.5.cloned.1.call-start = ((), (), s32[]{:S(2)}) async-start(), calls=%async_computation.5 | async-start | bytes 4718592 | tf_op jit(solution)/shard_map/psum | solution.py:189
  26.8 213.3 %copy-start.5 = (s32[768,8]{0,1:T(8,128)S(1)}, s32[768,8]{0,1:T(8,128)}, u32[]{:S(2)}) copy-start(s32[768,8]{0,1:T(8,128)} %param.8) | copy-start | bytes 73732
  26.8 213.3 %copy-start.6 = (s32[768,8]{0,1:T(8,128)S(1)}, s32[768,8]{0,1:T(8,128)}, u32[]{:S(2)}) copy-start(s32[768,8]{0,1:T(8,128)} %param.7) | copy-start | bytes 73732
  26.8 558.8 %all-gather.11.cloned.1.call-start = ((), (), s32[]{:S(2)}) async-start(), calls=%async_computation.8 | async-start | bytes 15728640 | tf_op jit(solution)/shard_map/all_gather | solution.py:178
  240.9 8.5 %all-to-all-start.2 = ((s32[4,1,3072]{2,1,0:T(1,128)}), s32[4,1,3072]{2,1,0:T(1,128)S(1)}, u32[]{:S(2)}, u32[]{:S(2)}) async-start(s32[4,1,3072]{2,1,0:T(1,128)} %copy.80), calls=%async_computation.2 | async-start | bytes 98304 | tf_op jit(solution)/shard_map/all_to_all | solution.py:170
  249.4 9.0 %all-to-all-start = ((s32[4,1,3072]{2,1,0:T(1,128)}), s32[4,1,3072]{2,1,0:T(1,128)S(1)}, u32[]{:S(2)}, u32[]{:S(2)}) async-start(s32[4,1,3072]{2,1,0:T(1,128)} %copy.76), calls=%async_computation | async-start | bytes 98304 | tf_op jit(solution)/shard_map/all_to_all | solution.py:170
  421.5 19.2 %all-to-all-start.1 = ((f32[4,1,3072]{2,1,0:T(1,128)}), f32[4,1,3072]{2,1,0:T(1,128)S(1)}, u32[]{:S(2)}, u32[]{:S(2)}) async-start(f32[4,1,3072]{2,1,0:T(1,128)} %copy.79), calls=%async_computation.1 | async-start | bytes 98304 | tf_op jit(solution)/shard_map/all_to_all | solution.py:170
  444.2 8.1 all-to-all-start.3
  452.3 14.2 %all-to-all-start.4 = ((f32[4,1,3072]{2,1,0:T(1,128)}), f32[4,1,3072]{2,1,0:T(1,128)S(1)}, u32[]{:S(2)}, u32[]{:S(2)}) async-start(f32[4,1,3072]{2,1,0:T(1,128)} %copy.91), calls=%async_computation.4 | async-start | bytes 98304 | tf_op jit(solution)/shard_map/all_to_all | solution.py:170
  486.8 149.2 %collective-permute-start.3 = (bf16[768,2048]{1,0:T(8,128)(2,1)}, bf16[768,2048]{1,0:T(8,128)(2,1)}, u32[]{:S(2)}, u32[]{:S(2)}) collective-permute-start(bf16[768,2048]{1,0:T(8,128)(2,1)} %shard_map.90), channel_id=1, source_target_pairs={{0,6},{2,4},{4,2},{6,0},{8,14},{10,12},{12,10},{14,8},{16,22},{18,... | collective-permute-start | bytes 9437192 | tf_op jit(solution)/shard_map/ppermute | solution.py:253
  502.8 156.7 %collective-permute-start.4 = (bf16[768,2048]{1,0:T(8,128)(2,1)}, bf16[768,2048]{1,0:T(8,128)(2,1)}, u32[]{:S(2)}, u32[]{:S(2)}) collective-permute-start(bf16[768,2048]{1,0:T(8,128)(2,1)} %shard_map.91), channel_id=1, source_target_pairs={{0,4},{2,6},{4,0},{6,2},{8,12},{10,14},{12,8},{14,10},{16,20},{18,... | collective-permute-start | bytes 9437192 | tf_op jit(solution)/shard_map/ppermute | solution.py:253
  521.7 137.8 %collective-permute-start.5 = (bf16[768,2048]{1,0:T(8,128)(2,1)}, bf16[768,2048]{1,0:T(8,128)(2,1)}, u32[]{:S(2)}, u32[]{:S(2)}) collective-permute-start(bf16[768,2048]{1,0:T(8,128)(2,1)} %shard_map.92), channel_id=1, source_target_pairs={{0,2},{2,0},{4,6},{6,4},{8,10},{10,8},{12,14},{14,12},{16,18},{18,... | collective-permute-start | bytes 9437192 | tf_op jit(solution)/shard_map/ppermute | solution.py:253
  601.6 92.4 %collective-permute-start = (bf16[768,2048]{1,0:T(8,128)(2,1)}, bf16[768,2048]{1,0:T(8,128)(2,1)}, u32[]{:S(2)}, u32[]{:S(2)}) collective-permute-start(bf16[768,2048]{1,0:T(8,128)(2,1)} %shard_map.86), channel_id=1, source_target_pairs={{0,6},{2,4},{4,2},{6,0},{8,14},{10,12},{12,10},{14,8},{16,22},{18,... | collective-permute-start | bytes 9437192 | tf_op jit(solution)/shard_map/ppermute | solution.py:262
  619.7 132.5 %collective-permute-start.1 = (bf16[768,2048]{1,0:T(8,128)(2,1)}, bf16[768,2048]{1,0:T(8,128)(2,1)}, u32[]{:S(2)}, u32[]{:S(2)}) collective-permute-start(bf16[768,2048]{1,0:T(8,128)(2,1)} %shard_map.87), channel_id=1, source_target_pairs={{0,4},{2,6},{4,0},{6,2},{8,12},{10,14},{12,8},{14,10},{16,20},{18,... | collective-permute-start | bytes 9437192 | tf_op jit(solution)/shard_map/ppermute | solution.py:262
  620.2 16.4 %copy-start.4 = (f32[768,768]{1,0:T(8,128)S(1)}, f32[768,768]{1,0:T(8,128)}, u32[]{:S(2)}) copy-start(f32[768,768]{1,0:T(8,128)} %all-reduce.5.cloned.1.call-done) | copy-start | bytes 7077892
  636.1 116.4 %collective-permute-start.2 = (bf16[768,2048]{1,0:T(8,128)(2,1)}, bf16[768,2048]{1,0:T(8,128)(2,1)}, u32[]{:S(2)}, u32[]{:S(2)}) collective-permute-start(bf16[768,2048]{1,0:T(8,128)(2,1)} %shard_map.88), channel_id=1, source_target_pairs={{0,2},{2,0},{4,6},{6,4},{8,10},{10,8},{12,14},{14,12},{16,18},{18,... | collective-permute-start | bytes 9437192 | tf_op jit(solution)/shard_map/ppermute | solution.py:262
  668.4 84.0 %copy-start.1 = (bf16[768,2048]{1,0:T(8,128)(2,1)S(1)}, bf16[768,2048]{1,0:T(8,128)(2,1)}, u32[]{:S(2)}) copy-start(bf16[768,2048]{1,0:T(8,128)(2,1)} %param.5) | copy-start | bytes 9437188
  804.6 5.0 copy-start.2
  804.6 6.7 copy-start.3
Sparse Core Ops, SparseCore 0:
  19.2 220.7 all-gather.6
  242.4 120.6 all-gather.8
  365.3 220.2 all-gather.10
Sparse Core Ops, SparseCore 1:
  26.9 23.9 all-reduce.4

commit v3 on v2

--- a/solution.py
+++ b/solution.py
@@ -172,8 +172,19 @@
         )
         return came.reshape(table.shape)
 
+    def partner_of(shift):
+        return [
+            (a * plane + b, a * plane + (b ^ shift)) for a in range(lines) for b in range(plane)
+        ]
+
+    def plane_order(table):
+        parts = [lax.dynamic_index_in_dim(table, here ^ k, 1) for k in range(plane)]
+        return jnp.concatenate(parts, axis=1)
+
     line_q = lax.all_gather(q_emb, "dp", axis_index_groups=line_groups)
-    plane_p = lax.all_gather(p_emb, "dp", axis_index_groups=plane_groups)
+    plane_p = jnp.stack(
+        [p_emb] + [lax.ppermute(p_emb, "dp", partner_of(shift)) for shift in range(1, plane)]
+    )
     p_later, _ = lax.optimization_barrier((p_emb, line_q))
     line_p = lax.all_gather(p_later, "dp", axis_index_groups=line_groups)
 
@@ -185,7 +196,10 @@
     line_wanted = exchange(wanted, line_groups)
     plane_wanted = exchange(wanted.transpose(1, 0, 2), plane_groups).transpose(0, 2, 1)
 
-    partial_scores = jnp.dot(q_emb, p_emb.T, preferred_element_type=jnp.float32) * scale
+    q_then, line_wanted, plane_wanted = lax.optimization_barrier(
+        (q_emb, line_wanted, plane_wanted)
+    )
+    partial_scores = jnp.dot(q_then, p_emb.T, preferred_element_type=jnp.float32) * scale
     scores = lax.psum(partial_scores, "group")
     near_part = pl.pallas_call(
         near_kernel,
@@ -199,8 +213,8 @@
         out_shape=jax.ShapeDtypeStruct((lines, rows, plane), jnp.float32),
         compiler_params=params(),
         cost_estimate=cost(n_data, rows, piece),
-    )(line_q, plane_p, line_wanted.transpose(0, 2, 1))
-    line_near = lax.psum(near_part.transpose(0, 2, 1) * scale, "group")
+    )(line_q, plane_p, plane_order(line_wanted).transpose(0, 2, 1))
+    line_near = plane_order(lax.psum(near_part.transpose(0, 2, 1) * scale, "group"))
     near = jnp.where(wanted >= 0, exchange(line_near, line_groups), -jnp.inf)
     near = near.reshape(n_data, rows)
 
@@ -222,11 +236,6 @@
 
     line_hard = exchange(hard, line_groups)
     plane_hard = exchange(hard.transpose(1, 0, 2), plane_groups).transpose(0, 2, 1)
-
-    def partner_of(shift):
-        return [
-            (a * plane + b, a * plane + (b ^ shift)) for a in range(lines) for b in range(plane)
-        ]
 
     def p_tables(target):
         asked = lax.dynamic_index_in_dim(line_wanted, target, 1, keepdims=True)
@@ -283,10 +292,15 @@
         jnp.bfloat16
     )
     gain_part = jnp.sum(grad_q * q_normed, axis=0) + jnp.sum(grad_p * p_normed, axis=0)
-    gain_full = lax.dynamic_update_slice_in_dim(
-        jnp.zeros((hidden,), jnp.float32), gain_part, member * piece, 0
-    )
-    loss_total, gain_total = lax.psum((loss_part, gain_full), ("dp", "group"))
+    chunk = piece // n_data
+    loss_column = jnp.full((n_data, 1), loss_part)
+    shares = jnp.concatenate([gain_part.reshape(n_data, chunk), loss_column], axis=1)
+    summed = jnp.sum(lax.all_to_all(shares, "dp", 0, 0, tiled=True), axis=0)
+    copies = jnp.broadcast_to(summed[None], (n_data * n_members, chunk + 1))
+    everyone = lax.all_to_all(copies, ("dp", "group"), 0, 0, tiled=True)
+    everyone = everyone.reshape(n_data, n_members, chunk + 1)
+    gain_total = everyone[:, :, :chunk].transpose(1, 0, 2).reshape(hidden)
+    loss_total = jnp.sum(everyone[0, :, chunk])
     count = rows * n_data
     return (grad_queries, grad_passages, gain_total / math.sqrt(count), loss_total / count)
 

time: 832 us -> 853 us (1.025)
  blocking collectives: 48.2 us -> 23.5 us
  starting transfers between devices: 25.5 us -> 41.5 us
  local copies, waits for them, and re-layouts: 21.7 us -> 35.9 us
  other arithmetic: 44.2 us -> 58.3 us
    ppermute x0 -> x3, waiting for transfers between devices: none -> 133 us  [local(): lax.ppermute(p_emb, 'dp', partner_of(shift))]
    all_gather x1 -> x0, waiting for transfers between devices: 103 us -> none  [local(): plane_p = lax.all_gather(p_emb, 'dp', axis_index_groups=plane_groups)]
    all_gather x1, waiting for transfers between devices: 63.4 us -> 0.01 us  [local(): line_p = lax.all_gather(p_later, 'dp', axis_index_groups=line_groups)]
    ppermute x3, waiting for transfers between devices: 64 us -> 102 us  [local(): q_parts.append(lax.ppermute(part, 'dp', partner_of(shift)))]
    ppermute x3, waiting for transfers between devices: 0.01 us -> 30.3 us  [local(): p_parts.append(lax.ppermute(part, 'dp', partner_of(shift)))]
    all_gather x1, waiting for transfers between devices: 213 us -> 187 us  [local(): line_q = lax.all_gather(q_emb, 'dp', axis_index_groups=line_groups)]
    psum x2 -> x1, blocking collectives: 43.1 us -> 18.4 us  [local(): lax.psum(near_part.transpose(0, 2, 1) * scale, 'group')]
    dynamic_slice x1 -> x11, local copies, waits for them, and re-layouts: 0.65 us -> 19.1 us  [the longest x6 15.3 us: plane_order(): parts = [lax.dynamic_index_in_dim(table, here ^ k, 1) for k in range(plane)]]
  transfers between devices with their start and end apart: 15 -> 19, of which waited for: 11 -> 11; matrix products, arithmetic and copies ran while one was open for 6% -> 9% of each run, Pallas kernels for 23% -> 22%
where the time goes in v3:
time: 853 us; the launch traced here: 845 us
  waiting for transfers between devices  476 us (56%)
  Pallas kernels  185 us (22%)
  other arithmetic  58.3 us (7%)
  starting transfers between devices  41.5 us (5%)
  local copies, waits for them, and re-layouts  35.9 us (4%)
  blocking collectives  23.5 us (3%)
  between operations  17.8 us (2%)
    all_gather x1, waiting for transfers between devices, local(): line_q = lax.all_gather(q_emb, 'dp', axis_index_groups=line_groups)  187 us
    ppermute x3, waiting for transfers between devices, local(): lax.ppermute(p_emb, 'dp', partner_of(shift))  133 us
    ppermute x3, waiting for transfers between devices, local(): q_parts.append(lax.ppermute(part, 'dp', partner_of(shift)))  102 us
    pallas_call x1, Pallas kernels, local(): pl.pallas_call(near_kernel, grid=(lines, plane), in_specs=[pl.BlockSpec((...  48.4 us
    pallas_call x3, Pallas kernels, local(): call(functools.partial(sent_p_kernel, scale), lines, p_specs, jnp.bfloat1...  48.1 us
    pallas_call x3, Pallas kernels, local(): call(sent_q_kernel, lines, q_specs, jnp.bfloat16, *size)  47.7 us
    ppermute x3, waiting for transfers between devices, local(): p_parts.append(lax.ppermute(part, 'dp', partner_of(shift)))  30.3 us
    all_to_all x5, waiting for transfers between devices, exchange(): lax.all_to_all(flat, 'dp', split_axis=0, concat_axis=0, axis_index_groups...  21.7 us
  transfers between devices with their start and end apart: 19, of which 11 were waited for; matrix products, arithmetic and copies ran while one was open for 9% of the time, Pallas kernels for 22%

profile of v3, /device:TPU:0, one launch (start us, length us, event | category | flops | bytes accessed | tf_op | source)
XLA Modules:
  0.0 844.8 jit_solution(6799682709643939339)
XLA Ops:
  14.7 4.9 fusion.8
  21.2 5.0 all-to-all-start.1
  26.9 4.1 all-to-all-done.1
  31.0 4.9 all-to-all-start
  36.1 11.5 %all-to-all-done = s32[4,1,3072]{2,1,0:T(1,128)S(1)} async-done(((s32[4,1,3072]{2,1,0:T(1,128)}), s32[4,1,3072]{2,1,0:T(1,128)S(1)}, u32[]{:S(2)}, u32[]{:S(2)}) %all-to-all-start) | async-done | bytes 49184 | tf_op jit(solution)/shard_map/all_to_all | solution.py:170
  47.8 6.9 convolution_multiply_fusion
  54.8 186.8 %all-gather.5.cloned.1.call-done = bf16[3072,2048]{1,0:T(8,128)(2,1)} async-done(((bf16[768,2048]{1,0:T(8,128)(2,1)}), bf16[3072,2048]{1,0:T(8,128)(2,1)}) %all-gather.5.cloned.1.call-update) | async-done | bytes 12582928 | tf_op jit(solution)/shard_map/all_gather | solution.py:184
  247.1 65.9 %collective-permute-done = bf16[768,2048]{1,0:T(8,128)(2,1)} collective-permute-done((bf16[768,2048]{1,0:T(8,128)(2,1)}, bf16[768,2048]{1,0:T(8,128)(2,1)}, u32[]{:S(2)}, u32[]{:S(2)}) %collective-permute-start) | collective-permute-done | bytes 3145760 | tf_op jit(solution)/shard_map/ppermute | solution.py:186
  313.0 67.6 %collective-permute-done.1 = bf16[768,2048]{1,0:T(8,128)(2,1)} collective-permute-done((bf16[768,2048]{1,0:T(8,128)(2,1)}, bf16[768,2048]{1,0:T(8,128)(2,1)}, u32[]{:S(2)}, u32[]{:S(2)}) %collective-permute-start.1) | collective-permute-done | bytes 3145760 | tf_op jit(solution)/shard_map/ppermute | solution.py:186
  380.6 10.5 %pad_maximum_fusion.p_ref = bf16[4,768,2048]{2,1,0:T(8,128)(2,1)} fusion(bf16[1,768,2048]{2,1,0:T(8,128)(2,1)} %bitcast.9, bf16[1,768,2048]{2,1,0:T(8,128)(2,1)} %bitcast.8, bf16[1,768,2048]{2,1,0:T(8,128)(2,1)} %bitcast.7, bf16[1,768,2048]{2,1,0:T(8,128)(2,1)} %bitcast.60), kind=kLoop, calls=%fused_computation | loop fusion | flops 18874368 | bytes 25165824 | tf_op jit(solution)/shard_map/stack | solution.py:185
  391.1 48.4 %shard_map.84 = f32[4,768,4]{2,1,0:T(8,128)} custom-call(bf16[4,768,2048]{2,1,0:T(8,128)(2,1)} %bitcast.75, bf16[4,768,2048]{2,1,0:T(8,128)(2,1)} %pad_maximum_fusion.p_ref, s32[4,768,4]{2,1,0:T(8,128)} %copy.87.wanted_ref), custom_call_target="tpu_custom_call" | custom-call | flops 38654705664 | bytes 50331648 | tf_op jit(solution)/shard_map/pallas_call | solution.py:204
  442.1 18.4 %psum.45 = f32[4,4,768]{1,2,0:T(8,128)} all-reduce(f32[4,4,768]{1,2,0:T(8,128)} %multiply_bitcast_fusion), channel_id=1, replica_groups=mesh['dp'=16,'group'=2] {'group'}, use_global_device_ids=true, to_apply=%region_7.8 | all-reduce | flops 12288 | bytes 98304 | tf_op jit(solution)/shard_map/psum | solution.py:217
  460.6 7.7 constant_dynamic-slice_fusion.11
  493.6 3.4 all-to-all-done.3
  497.0 5.0 all-to-all-start.4
  512.1 16.1 %shard_map.90 = bf16[768,2048]{1,0:T(8,128)(2,1)} custom-call(bf16[4,768,2048]{2,1,0:T(8,128)(2,1)} %bitcast.76, s32[4,1,768]{2,1,0:T(1,128)} %copy-done.9, f32[768,4]{1,0:T(8,128)} %get-tuple-element.28.hard_ref), custom_call_target="tpu_custom_call" | custom-call | flops 9663676416 | bytes 12582912 | tf_op jit(solution)/shard_map/pallas_call | solution.py:259
  528.8 16.0 %shard_map.91 = bf16[768,2048]{1,0:T(8,128)(2,1)} custom-call(bf16[4,768,2048]{2,1,0:T(8,128)(2,1)} %bitcast.77, s32[4,1,768]{2,1,0:T(1,128)} %copy-done.8, f32[768,4]{1,0:T(8,128)} %get-tuple-element.30.hard_ref), custom_call_target="tpu_custom_call" | custom-call | flops 9663676416 | bytes 12582912 | tf_op jit(solution)/shard_map/pallas_call | solution.py:259
  546.4 16.0 %shard_map.92 = bf16[768,2048]{1,0:T(8,128)(2,1)} custom-call(bf16[4,768,2048]{2,1,0:T(8,128)(2,1)} %bitcast.78, s32[4,1,768]{2,1,0:T(1,128)} %copy-done.7, f32[768,4]{1,0:T(8,128)} %get-tuple-element.29.hard_ref), custom_call_target="tpu_custom_call" | custom-call | flops 9663676416 | bytes 12582912 | tf_op jit(solution)/shard_map/pallas_call | solution.py:259
  563.7 16.1 %shard_map.86 = bf16[768,2048]{1,0:T(8,128)(2,1)} custom-call(bf16[4,768,2048]{2,1,0:T(8,128)(2,1)} %bitcast.80, s32[768,4]{1,0:T(8,128)} %bitcast.66, f32[768,4]{1,0:T(8,128)} %bitcast.69), custom_call_target="tpu_custom_call" | custom-call | flops 9663676416 | bytes 12582912 | tf_op jit(solution)/shard_map/pallas_call | solution.py:268
  580.4 15.7 %shard_map.87 = bf16[768,2048]{1,0:T(8,128)(2,1)} custom-call(bf16[4,768,2048]{2,1,0:T(8,128)(2,1)} %bitcast.81, s32[768,4]{1,0:T(8,128)} %bitcast.65, f32[768,4]{1,0:T(8,128)} %bitcast.68), custom_call_target="tpu_custom_call" | custom-call | flops 9663676416 | bytes 12582912 | tf_op jit(solution)/shard_map/pallas_call | solution.py:268
  597.7 15.8 %shard_map.88 = bf16[768,2048]{1,0:T(8,128)(2,1)} custom-call(bf16[4,768,2048]{2,1,0:T(8,128)(2,1)} %bitcast.82, s32[768,4]{1,0:T(8,128)} %bitcast.64, f32[768,4]{1,0:T(8,128)} %bitcast.67), custom_call_target="tpu_custom_call" | custom-call | flops 9663676416 | bytes 12582912 | tf_op jit(solution)/shard_map/pallas_call | solution.py:268
  617.2 20.4 %shard_map.89 = f32[768,2048]{1,0:T(8,128)} custom-call(bf16[768,768]{1,0:T(8,128)(2,1)} %subtract_convert_fusion.weights_ref, bf16[768,2048]{1,0:T(8,128)(2,1)} %get-tuple-element.8.own_ref, bf16[4,768,2048]{2,1,0:T(8,128)(2,1)} %bitcast.79, s32[4,1,768]{2,1,0:T(1,128)} %copy-done.6, f32[768,4]{1,0:T(8,128)} %get-tuple-element.31.hard_ref), custom_call_target="tpu_custom_call" | custom-call | flops 9663676416 | bytes 12582912 | tf_op jit(solution)/shard_map/pallas_call | solution.py:263
  637.6 30.3 %collective-permute-done.7 = bf16[768,2048]{1,0:T(8,128)(2,1)} collective-permute-done((bf16[768,2048]{1,0:T(8,128)(2,1)}, bf16[768,2048]{1,0:T(8,128)(2,1)}, u32[]{:S(2)}, u32[]{:S(2)}) %collective-permute-start.7) | collective-permute-done | bytes 3145760 | tf_op jit(solution)/shard_map/ppermute | solution.py:262
  668.0 8.9 %fusion.20 = (f32[2048]{0:T(1024)S(1)}, f32[768]{0:T(1024)S(1)}, f32[768,2048]{1,0:T(8,128)}) fusion(bf16[768,2048]{1,0:T(8,128)(2,1)S(1)} %copy-done, f32[768]{0:T(1024)S(1)} %get-tuple-element.50, f32[2048]{0:T(1024)S(1)} %get-tuple-element.27, bf16[768,2048]{1,0:T(8,128)(2,1)} %collective-permute-done.8, bf16[768,2048]{1,0:T(8,128)(2,1)} %collective-permute-done.7, ...), kind=kLoop, calls=%fused_computation.25 | loop fusion | flops 20444416 | bytes 25188352 | tf_op jit(solution)/shard_map/reduce_sum | solution.py:294
  676.9 20.0 %shard_map.85 = f32[768,2048]{1,0:T(8,128)} custom-call(bf16[768,768]{1,0:T(8,128)(2,1)} %subtract_convert_fusion.weights_ref, bf16[768,2048]{1,0:T(8,128)(2,1)} %get-tuple-element.10.own_ref, bf16[4,768,2048]{2,1,0:T(8,128)(2,1)} %bitcast.83, s32[768,4]{1,0:T(8,128)} %bitcast.63, f32[768,4]{1,0:T(8,128)} %bitcast.70), custom_call_target="tpu_custom_call" | custom-call | flops 9663676416 | bytes 12582912 | tf_op jit(solution)/shard_map/pallas_call | solution.py:272
  696.9 38.5 %collective-permute-done.3 = bf16[768,2048]{1,0:T(8,128)(2,1)} collective-permute-done((bf16[768,2048]{1,0:T(8,128)(2,1)}, bf16[768,2048]{1,0:T(8,128)(2,1)}, u32[]{:S(2)}, u32[]{:S(2)}) %collective-permute-start.3) | collective-permute-done | bytes 3145760 | tf_op jit(solution)/shard_map/ppermute | solution.py:271
  735.4 63.9 %collective-permute-done.4 = bf16[768,2048]{1,0:T(8,128)(2,1)} collective-permute-done((bf16[768,2048]{1,0:T(8,128)(2,1)}, bf16[768,2048]{1,0:T(8,128)(2,1)}, u32[]{:S(2)}, u32[]{:S(2)}) %collective-permute-start.4) | collective-permute-done | bytes 3145760 | tf_op jit(solution)/shard_map/ppermute | solution.py:271
  799.3 8.9 %fusion.13 = (f32[2048]{0:T(1024)S(1)}, f32[768]{0:T(1024)S(1)}, f32[768,2048]{1,0:T(8,128)}) fusion(bf16[768,2048]{1,0:T(8,128)(2,1)S(1)} %copy-done.1, f32[768]{0:T(1024)S(1)} %copy-done.5, f32[2048]{0:T(1024)S(1)} %copy-done.3, bf16[768,2048]{1,0:T(8,128)(2,1)} %collective-permute-done.5, bf16[768,2048]{1,0:T(8,128)(2,1)} %collective-permute-done.4, ...), kind=kLoop, calls=%fused_computation.18 | loop fusion | flops 22017280 | bytes 25188352 | tf_op jit(solution)/shard_map/reduce_sum | solution.py:294
  809.5 3.5 all-to-all-start.5
  815.5 4.8 fusion.19
  821.0 5.8 all-to-all-start.6
  826.9 5.7 fusion.12
  (123 shorter events, 69.4 us)
Async XLA Ops:
  8.0 2.8 copy-start
  8.0 233.6 %all-gather.5.cloned.1.call-start = ((), (), s32[]{:S(2)}) async-start(), calls=%async_computation.8 | async-start | bytes 15728640 | tf_op jit(solution)/shard_map/all_gather | solution.py:184
  8.1 3.5 copy-start.12
  14.7 4.9 copy-start.4
  19.6 0.7 copy-start.10
  19.6 0.8 copy-start.11
  21.2 9.8 %all-to-all-start.1 = ((s32[4,1,3072]{2,1,0:T(1,128)}), s32[4,1,3072]{2,1,0:T(1,128)S(1)}, u32[]{:S(2)}, u32[]{:S(2)}) async-start(s32[4,1,3072]{2,1,0:T(1,128)} %copy.86), calls=%async_computation.1 | async-start | bytes 98304 | tf_op jit(solution)/shard_map/all_to_all | solution.py:170
  31.0 16.6 %all-to-all-start = ((s32[4,1,3072]{2,1,0:T(1,128)}), s32[4,1,3072]{2,1,0:T(1,128)S(1)}, u32[]{:S(2)}, u32[]{:S(2)}) async-start(s32[4,1,3072]{2,1,0:T(1,128)} %copy.85), calls=%async_computation | async-start | bytes 98304 | tf_op jit(solution)/shard_map/all_to_all | solution.py:170
  35.9 447.7 %all-reduce.5.cloned.1.call-start = ((), (), s32[]{:S(2)}) async-start(), calls=%async_computation.7 | async-start | bytes 4718592 | tf_op jit(solution)/shard_map/psum | solution.py:203
  54.8 508.9 %all-gather.7.cloned.1.call-start = ((), (), s32[]{:S(2)}) async-start(), calls=%async_computation.9 | async-start | bytes 15728640 | tf_op jit(solution)/shard_map/all_gather | solution.py:189
  241.7 71.3 %collective-permute-start = (bf16[768,2048]{1,0:T(8,128)(2,1)}, bf16[768,2048]{1,0:T(8,128)(2,1)}, u32[]{:S(2)}, u32[]{:S(2)}) collective-permute-start(bf16[768,2048]{1,0:T(8,128)(2,1)} %get-tuple-element.10.own_ref), channel_id=1, source_target_pairs={{0,2},{2,0},{4,6},{6,4},{8,10},{10,8},{12,14},{14,12},{16,18},{18,... | collective-permute-start | bytes 9437192 | tf_op jit(solution)/shard_map/ppermute | solution.py:186
  243.0 137.5 %collective-permute-start.1 = (bf16[768,2048]{1,0:T(8,128)(2,1)}, bf16[768,2048]{1,0:T(8,128)(2,1)}, u32[]{:S(2)}, u32[]{:S(2)}) collective-permute-start(bf16[768,2048]{1,0:T(8,128)(2,1)} %get-tuple-element.10.own_ref), channel_id=1, source_target_pairs={{0,4},{2,6},{4,0},{6,2},{8,12},{10,14},{12,8},{14,10},{16,20},{18,... | collective-permute-start | bytes 9437192 | tf_op jit(solution)/shard_map/ppermute | solution.py:186
  244.2 136.4 %collective-permute-start.2 = (bf16[768,2048]{1,0:T(8,128)(2,1)}, bf16[768,2048]{1,0:T(8,128)(2,1)}, u32[]{:S(2)}, u32[]{:S(2)}) collective-permute-start(bf16[768,2048]{1,0:T(8,128)(2,1)} %get-tuple-element.10.own_ref), channel_id=1, source_target_pairs={{0,6},{2,4},{4,2},{6,0},{8,14},{10,12},{12,10},{14,8},{16,22},{18,... | collective-permute-start | bytes 9437192 | tf_op jit(solution)/shard_map/ppermute | solution.py:186
  245.3 145.8 %copy-start.6 = (s32[4,1,768]{2,1,0:T(1,128)}, s32[4,1,768]{2,1,0:T(1,128)S(1)}, u32[]{:S(2)}) copy-start(s32[4,1,768]{2,1,0:T(1,128)S(1)} %get-tuple-element.44.asked_ref) | copy-start | bytes 36868
  245.3 145.8 %copy-start.7 = (s32[4,1,768]{2,1,0:T(1,128)}, s32[4,1,768]{2,1,0:T(1,128)S(1)}, u32[]{:S(2)}) copy-start(s32[4,1,768]{2,1,0:T(1,128)S(1)} %get-tuple-element.47.asked_ref) | copy-start | bytes 36868
  245.3 145.8 %copy-start.8 = (s32[4,1,768]{2,1,0:T(1,128)}, s32[4,1,768]{2,1,0:T(1,128)S(1)}, u32[]{:S(2)}) copy-start(s32[4,1,768]{2,1,0:T(1,128)S(1)} %get-tuple-element.46.asked_ref) | copy-start | bytes 36868
  245.3 145.8 %copy-start.9 = (s32[4,1,768]{2,1,0:T(1,128)}, s32[4,1,768]{2,1,0:T(1,128)S(1)}, u32[]{:S(2)}) copy-start(s32[4,1,768]{2,1,0:T(1,128)S(1)} %get-tuple-element.45.asked_ref) | copy-start | bytes 36868
  476.5 9.0 %all-to-all-start.2 = ((f32[4,1,3072]{2,1,0:T(1,128)}), f32[4,1,3072]{2,1,0:T(1,128)S(1)}, u32[]{:S(2)}, u32[]{:S(2)}) async-start(f32[4,1,3072]{2,1,0:T(1,128)} %all_to_all.52), calls=%async_computation.2 | async-start | bytes 98304 | tf_op jit(solution)/shard_map/all_to_all | solution.py:170
  489.0 8.1 all-to-all-start.3
  497.0 10.7 %all-to-all-start.4 = ((f32[4,1,3072]{2,1,0:T(1,128)}), f32[4,1,3072]{2,1,0:T(1,128)S(1)}, u32[]{:S(2)}, u32[]{:S(2)}) async-start(f32[4,1,3072]{2,1,0:T(1,128)} %copy.103), calls=%async_computation.4 | async-start | bytes 98304 | tf_op jit(solution)/shard_map/all_to_all | solution.py:170
  528.2 85.3 %collective-permute-start.6 = (bf16[768,2048]{1,0:T(8,128)(2,1)}, bf16[768,2048]{1,0:T(8,128)(2,1)}, u32[]{:S(2)}, u32[]{:S(2)}) collective-permute-start(bf16[768,2048]{1,0:T(8,128)(2,1)} %shard_map.90), channel_id=1, source_target_pairs={{0,6},{2,4},{4,2},{6,0},{8,14},{10,12},{12,10},{14,8},{16,22},{18,... | collective-permute-start | bytes 9437192 | tf_op jit(solution)/shard_map/ppermute | solution.py:262
  544.8 123.2 %collective-permute-start.7 = (bf16[768,2048]{1,0:T(8,128)(2,1)}, bf16[768,2048]{1,0:T(8,128)(2,1)}, u32[]{:S(2)}, u32[]{:S(2)}) collective-permute-start(bf16[768,2048]{1,0:T(8,128)(2,1)} %shard_map.91), channel_id=1, source_target_pairs={{0,4},{2,6},{4,0},{6,2},{8,12},{10,14},{12,8},{14,10},{16,20},{18,... | collective-permute-start | bytes 9437192 | tf_op jit(solution)/shard_map/ppermute | solution.py:262
  562.4 105.6 %collective-permute-start.8 = (bf16[768,2048]{1,0:T(8,128)(2,1)}, bf16[768,2048]{1,0:T(8,128)(2,1)}, u32[]{:S(2)}, u32[]{:S(2)}) collective-permute-start(bf16[768,2048]{1,0:T(8,128)(2,1)} %shard_map.92), channel_id=1, source_target_pairs={{0,2},{2,0},{4,6},{6,4},{8,10},{10,8},{12,14},{14,12},{16,18},{18,... | collective-permute-start | bytes 9437192 | tf_op jit(solution)/shard_map/ppermute | solution.py:262
  579.8 155.6 %collective-permute-start.3 = (bf16[768,2048]{1,0:T(8,128)(2,1)}, bf16[768,2048]{1,0:T(8,128)(2,1)}, u32[]{:S(2)}, u32[]{:S(2)}) collective-permute-start(bf16[768,2048]{1,0:T(8,128)(2,1)} %shard_map.86), channel_id=1, source_target_pairs={{0,6},{2,4},{4,2},{6,0},{8,14},{10,12},{12,10},{14,8},{16,22},{18,... | collective-permute-start | bytes 9437192 | tf_op jit(solution)/shard_map/ppermute | solution.py:271
  596.1 203.2 %collective-permute-start.4 = (bf16[768,2048]{1,0:T(8,128)(2,1)}, bf16[768,2048]{1,0:T(8,128)(2,1)}, u32[]{:S(2)}, u32[]{:S(2)}) collective-permute-start(bf16[768,2048]{1,0:T(8,128)(2,1)} %shard_map.87), channel_id=1, source_target_pairs={{0,4},{2,6},{4,0},{6,2},{8,12},{10,14},{12,8},{14,10},{16,20},{18,... | collective-permute-start | bytes 9437192 | tf_op jit(solution)/shard_map/ppermute | solution.py:271
  597.7 17.2 %copy-start.2 = (f32[768,768]{1,0:T(8,128)S(1)}, f32[768,768]{1,0:T(8,128)}, u32[]{:S(2)}) copy-start(f32[768,768]{1,0:T(8,128)} %all-reduce.5.cloned.1.call-done) | copy-start | bytes 7077892
  613.5 185.7 %collective-permute-start.5 = (bf16[768,2048]{1,0:T(8,128)(2,1)}, bf16[768,2048]{1,0:T(8,128)(2,1)}, u32[]{:S(2)}, u32[]{:S(2)}) collective-permute-start(bf16[768,2048]{1,0:T(8,128)(2,1)} %shard_map.88), channel_id=1, source_target_pairs={{0,2},{2,0},{4,6},{6,4},{8,10},{10,8},{12,14},{14,12},{16,18},{18,... | collective-permute-start | bytes 9437192 | tf_op jit(solution)/shard_map/ppermute | solution.py:271
  676.9 122.4 %copy-start.1 = (bf16[768,2048]{1,0:T(8,128)(2,1)S(1)}, bf16[768,2048]{1,0:T(8,128)(2,1)}, u32[]{:S(2)}) copy-start(bf16[768,2048]{1,0:T(8,128)(2,1)} %param.5) | copy-start | bytes 9437188
  676.9 122.4 %copy-start.3 = (f32[2048]{0:T(1024)S(1)}, f32[2048]{0:T(1024)}, u32[]{:S(2)}) copy-start(f32[2048]{0:T(1024)} %get-tuple-element.26) | copy-start | bytes 24580
  676.9 122.4 %copy-start.5 = (f32[768]{0:T(1024)S(1)}, f32[768]{0:T(1024)}, u32[]{:S(2)}) copy-start(f32[768]{0:T(1024)} %copy-done.4) | copy-start | bytes 9220
  809.5 10.9 %all-to-all-start.5 = ((f32[16,1,129]{2,1,0:T(1,128)}), f32[16,1,129]{2,1,0:T(1,128)S(1)}, u32[]{:S(2)}, u32[]{:S(2)}) async-start(f32[16,1,129]{2,1,0:T(1,128)} %all_to_all.47), calls=%async_computation.5 | async-start | bytes 32768 | tf_op jit(solution)/shard_map/all_to_all | solution.py:298
  821.0 13.1 %all-to-all-start.6 = ((f32[32,1,129]{2,1,0:T(1,128)}), f32[32,1,129]{2,1,0:T(1,128)S(1)}, u32[]{:S(2)}, u32[]{:S(2)}) async-start(f32[32,1,129]{2,1,0:T(1,128)} %broadcast_in_dim.32), calls=%async_computation.6 | async-start | bytes 65536 | tf_op jit(solution)/shard_map/all_to_all | solution.py:300
Sparse Core Ops, SparseCore 0:
  19.8 221.8 all-gather.4
  243.8 215.8 all-gather.6
Sparse Core Ops, SparseCore 1:
  54.8 18.9 all-reduce.4
